TPU v7x, 256 devices: a whole 4x4x8 slice. The times are simulated.
256 devices in a mesh: dp: 16 (over y_lo, z), tensor: 16 (over x, y_hi, core).
Axes of the slice: x: 4, y: 4 (y_hi: 2, y_lo: 2; y = y_hi * 2 + y_lo), z: 8, core: 2. Of those that a mesh axis runs over, the one named last changes fastest.
Arguments:
- tokens: bfloat16 [4096, 5120], P('dp', 'tensor'), may hold values from -6 to 6
- upstream: bfloat16 [4096, 5120], P('dp', 'tensor'), may hold values from -6 to 6
- gate_weight: bfloat16 [5120, 8192], P('dp', 'tensor'), may hold values from -0.078125 to 0.078125
- up_weight: bfloat16 [5120, 8192], P('dp', 'tensor'), may hold values from -0.078125 to 0.078125
- down_weight: bfloat16 [5120, 8192], P('dp', 'tensor'), may hold values from -0.0625 to 0.0625
- adapter_a: bfloat16 [5120, 128], replicated, may hold values from -0.078125 to 0.078125
- adapter_b: bfloat16 [128, 8192], P(None, 'tensor'), may hold values from -0.75 to 0.75
- membership: int32 [4096], P('dp'), may hold values from 0 to 255, as said below
Outputs:
- log_ratio: float32 [4096], P('dp')
- input_grad: bfloat16 [4096, 5120], P('dp', 'tensor')
- adapter_b_gradient: float32 [128, 8192], P('dp', 'tensor')
Inputs may be any that keep to these rules, and one draw needn't show every extreme that they name: `membership`: each aligned block of 256 rows holds every number 0 to 255 once.
All inputs are finite; a program needn't handle non-finite values.
Results may differ from a plain program's by a relative error of at most 0.022.
Values may be sent and summed in bfloat16 or wider, within the bound.
A program may use at most 128 MiB of HBM per device.

v0:
```python
import math

import jax
import jax.numpy as jnp
from jax import lax
from jax.sharding import PartitionSpec as P

adapter_scale = 0.5
beta_coef = 0.5
loss_scale = 128.0


def transposed_product(left, right):
    return lax.dot_general(
        left, right, (((1,), (1,)), ((), ())), preferred_element_type=jnp.float32
    )


def lowrank_product(left, right):
    return lax.dot_general(
        left, right, (((0,), (0,)), ((), ())), preferred_element_type=jnp.float32
    )


def on_device(
    tokens, upstream, gate_weight, up_weight, down_weight, adapter_a, adapter_b, membership
):
    x_full, u_full = (
        lax.all_gather(tokens, "tensor", axis=1, tiled=True),
        lax.all_gather(upstream, "tensor", axis=1, tiled=True),
    )
    n_rows = x_full.shape[0]
    width = x_full.shape[1]
    rank = adapter_b.shape[0] // 2
    w_gate, w_up, w_down = (
        lax.all_gather(gate_weight, "dp", axis=0, tiled=True),
        lax.all_gather(up_weight, "dp", axis=0, tiled=True),
        lax.all_gather(down_weight, "dp", axis=0, tiled=True),
    )
    gate_activation = jnp.dot(x_full, w_gate, preferred_element_type=jnp.float32)
    up_activation = jnp.dot(x_full, w_up, preferred_element_type=jnp.float32)
    readout = jnp.dot(u_full, w_down, preferred_element_type=jnp.float32)
    low = jnp.dot(x_full, adapter_a, preferred_element_type=jnp.float32).astype(jnp.bfloat16)
    gate_lowrank = low[:, :rank]
    up_lowrank = low[:, rank:]
    gate_adapter_right = adapter_b[:rank]
    up_adapter_right = adapter_b[rank:]
    policy_gate = gate_activation + adapter_scale * jnp.dot(
        gate_lowrank, gate_adapter_right, preferred_element_type=jnp.float32
    )
    policy_up = up_activation + adapter_scale * jnp.dot(
        up_lowrank, up_adapter_right, preferred_element_type=jnp.float32
    )
    shift = jax.nn.silu(policy_gate) * policy_up - jax.nn.silu(gate_activation) * up_activation
    partial_ratio = jnp.sum(shift * readout, axis=1)
    log_ratio = lax.psum(partial_ratio, "tensor") / math.sqrt(width)
    side = (1 - 2 * (membership % 2)).astype(jnp.float32)
    pair_index = membership // 2
    columns = jnp.arange(n_rows // 2, dtype=jnp.int32)
    onehot = (pair_index[:, None] == columns[None, :]).astype(jnp.float32)
    link = jnp.exp(log_ratio) + log_ratio
    margin = beta_coef * jnp.dot(side * link, onehot, precision=lax.Precision.HIGHEST)
    pair_weight = -loss_scale * beta_coef * jax.nn.sigmoid(-margin)
    per_row = jnp.dot(onehot, pair_weight, precision=lax.Precision.HIGHEST)
    coeff = per_row * side * (jnp.exp(log_ratio) + 1.0)
    d_hidden = coeff[:, None] * readout / math.sqrt(width)
    sig = jax.nn.sigmoid(policy_gate)
    dsilu = sig * (1.0 + policy_gate * (1.0 - sig))
    gate_gradient = (d_hidden * policy_up * dsilu).astype(jnp.bfloat16)
    up_gradient = (d_hidden * policy_gate * sig).astype(jnp.bfloat16)
    lowrank_gradient = (
        adapter_scale
        * jnp.concatenate(
            [
                transposed_product(gate_gradient, gate_adapter_right),
                transposed_product(up_gradient, up_adapter_right),
            ],
            axis=1,
        )
    ).astype(jnp.bfloat16)
    adapter_term = transposed_product(lowrank_gradient, adapter_a)
    terms = (
        transposed_product(gate_gradient, w_gate)
        + transposed_product(up_gradient, w_up)
        + adapter_term
    )
    input_grad = lax.psum_scatter(
        terms.astype(jnp.bfloat16), "tensor", scatter_dimension=1, tiled=True
    )
    gradient_pieces = adapter_scale * jnp.concatenate(
        [lowrank_product(gate_lowrank, gate_gradient), lowrank_product(up_lowrank, up_gradient)],
        axis=0,
    )
    adapter_b_gradient = lax.psum_scatter(
        gradient_pieces.astype(jnp.bfloat16), "dp", scatter_dimension=0, tiled=True
    ).astype(jnp.float32)
    return (log_ratio, input_grad, adapter_b_gradient)


def solution(mesh):
    placed = (
        P("dp", "tensor"),
        P("dp", "tensor"),
        P("dp", "tensor"),
        P("dp", "tensor"),
        P("dp", "tensor"),
        P(),
        P(None, "tensor"),
        P("dp"),
    )
    return jax.shard_map(
        on_device,
        mesh=mesh,
        in_specs=placed,
        out_specs=(P("dp"), P("dp", "tensor"), P("dp", "tensor")),
        check_vma=False,
    )
```

profile of v0, /device:TPU:1, one launch (start us, length us, event | category | flops | bytes accessed | tf_op | source)
XLA Modules:
  0.0 556.4 jit_solution(4374426679236373669)
XLA Ops:
  7.2 0.7 all-gather.6.cloned.1.call-update
  8.0 0.7 all-gather.8.cloned.1.call-update
  8.7 0.7 all-gather.10.cloned.1.call-update
  9.4 0.5 all-gather.12.cloned.1.call-update
  10.0 0.5 all-gather.14.cloned.1.call-update
  10.6 0.7 and_select_fusion.1
  11.3 59.2 %all-gather.6.cloned.1.call-done = bf16[256,5120]{0,1:T(8,128)(2,1)} async-done(((bf16[256,320]{0,1:T(8,128)(2,1)}), bf16[256,5120]{0,1:T(8,128)(2,1)}) %all-gather.6.cloned.1.call-update) | async-done | bytes 2621456 | tf_op jit(solution)/shard_map/all_gather | solution.py:29
  70.5 2.4 convolution_convert_fusion
  72.9 69.2 %all-gather.8.cloned.1.call-done = bf16[5120,512]{1,0:T(8,128)(2,1)} async-done(((bf16[320,512]{1,0:T(8,128)(2,1)}), bf16[5120,512]{1,0:T(8,128)(2,1)}) %all-gather.8.cloned.1.call-update) | async-done | bytes 5242896 | tf_op jit(solution)/shard_map/all_gather | solution.py:36
  142.1 4.8 fusion.34
  147.0 0.3 fusion.1
  147.2 72.5 %all-gather.10.cloned.1.call-done = bf16[5120,512]{1,0:T(8,128)(2,1)} async-done(((bf16[320,512]{1,0:T(8,128)(2,1)}), bf16[5120,512]{1,0:T(8,128)(2,1)}) %all-gather.10.cloned.1.call-update) | async-done | bytes 5242896 | tf_op jit(solution)/shard_map/all_gather | solution.py:37
  219.8 4.8 fusion.35
  224.6 0.2 fusion.2
  224.9 57.7 %all-gather.12.cloned.1.call-done = bf16[256,5120]{0,1:T(8,128)(2,1)} async-done(((bf16[256,320]{0,1:T(8,128)(2,1)}), bf16[256,5120]{0,1:T(8,128)(2,1)}) %all-gather.12.cloned.1.call-update) | async-done | bytes 2621456 | tf_op jit(solution)/shard_map/all_gather | solution.py:30
  282.6 71.5 %all-gather.14.cloned.1.call-done = bf16[5120,512]{1,0:T(8,128)(2,1)} async-done(((bf16[320,512]{1,0:T(8,128)(2,1)}), bf16[5120,512]{1,0:T(8,128)(2,1)}) %all-gather.14.cloned.1.call-update) | async-done | bytes 5242896 | tf_op jit(solution)/shard_map/all_gather | solution.py:38
  354.1 5.8 %multiply_reduce_fusion = (f32[256]{0:T(256)S(1)}, f32[256,512]{1,0:T(8,128)}) fusion(f32[256,512]{1,0:T(8,128)S(1)} %fusion.35, f32[256,512]{1,0:T(8,128)S(1)} %fusion.34, f32[256,512]{1,0:T(8,128)S(1)} %fusion.2, f32[256,512]{1,0:T(8,128)S(1)} %fusion.1, bf16[256,5120]{0,1:T(8,128)(2,1)} %all-gather.12.cloned.1.call-done, ...), kind=kOutput, calls=%fused_computation.18 | convolution fusion | flops 1343880960 | bytes 10486784 | tf_op jit(solution)/shard_map/dot_general | solution.py:42
  359.9 40.8 %psum.7 = f32[256]{0:T(256)S(1)} all-reduce(f32[256]{0:T(256)S(1)} %get-tuple-element.7), channel_id=1, replica_groups=mesh['dp'=16,'tensor'=16] {'tensor'}, use_global_device_ids=true, to_apply=%region_1.2 | all-reduce | flops 256 | bytes 2048 | tf_op jit(solution)/shard_map/psum | solution.py:56
  400.8 0.2 fusion.8
  401.0 0.2 fusion.11
  401.3 1.3 multiply_convert_fusion
  402.6 0.2 fusion.16
  402.8 0.9 fusion.22
  403.7 0.2 fusion.19
  404.0 0.9 fusion.25
  404.9 0.7 fusion.9
  405.6 4.0 fusion.36
  409.7 4.1 convolution_add_fusion.1
  413.8 2.4 fusion
  416.2 40.1 %reduce-scatter.5.cloned.1.call-done = bf16[8,512]{1,0:T(8,128)(2,1)} async-done(((bf16[128,512]{1,0:T(8,128)(2,1)}), bf16[8,512]{1,0:T(8,128)(2,1)}) %reduce-scatter.5.cloned.1.call-update) | async-done | bytes 8208 | tf_op jit(solution)/shard_map/reduce_scatter | solution.py:94
  456.3 1.3 convert_element_type.32
  457.6 92.0 %reduce-scatter.3.cloned.1.call-done = bf16[256,320]{0,1:T(8,128)(2,1)} async-done(((bf16[256,5120]{0,1:T(8,128)(2,1)}), bf16[256,320]{0,1:T(8,128)(2,1)}) %reduce-scatter.3.cloned.1.call-update) | async-done | bytes 163856 | tf_op jit(solution)/shard_map/reduce_scatter | solution.py:87
  (23 shorter events, 0.4 us)
Async XLA Ops:
  7.2 63.3 %copy-start = (bf16[5120,128]{1,0:T(8,128)(2,1)S(1)}, bf16[5120,128]{1,0:T(8,128)(2,1)}, u32[]{:S(2)}) copy-start(bf16[5120,128]{1,0:T(8,128)(2,1)} %param.13) | copy-start | bytes 3932164
  7.2 63.3 %all-gather.6.cloned.1.call-start = ((), (), s32[]{:S(2)}) async-start(), calls=%async_computation.2 | async-start | bytes 2785280 | tf_op jit(solution)/shard_map/all_gather | solution.py:29
  7.9 134.2 %all-gather.8.cloned.1.call-start = ((), (), s32[]{:S(2)}) async-start(), calls=%async_computation.3 | async-start | bytes 5570560 | tf_op jit(solution)/shard_map/all_gather | solution.py:36
  8.7 211.1 %all-gather.10.cloned.1.call-start = ((), (), s32[]{:S(2)}) async-start(), calls=%async_computation.4 | async-start | bytes 5570560 | tf_op jit(solution)/shard_map/all_gather | solution.py:37
  9.4 273.2 %all-gather.12.cloned.1.call-start = ((), (), s32[]{:S(2)}) async-start(), calls=%async_computation.5 | async-start | bytes 2785280 | tf_op jit(solution)/shard_map/all_gather | solution.py:30
  10.0 344.2 %all-gather.14.cloned.1.call-start = ((), (), s32[]{:S(2)}) async-start(), calls=%async_computation.6 | async-start | bytes 5570560 | tf_op jit(solution)/shard_map/all_gather | solution.py:38
  10.6 445.8 %reduce-scatter.5.cloned.1.call-start = ((), (), s32[]{:S(2)}) async-start(), calls=%async_computation.8 | async-start | bytes 139264 | tf_op jit(solution)/shard_map/reduce_scatter | solution.py:94
  72.9 74.1 %copy-start.2 = (bf16[256,128]{0,1:T(8,128)(2,1)}, bf16[256,128]{0,1:T(8,128)(2,1)S(1)}, u32[]{:S(2)}) copy-start(bf16[256,128]{0,1:T(8,128)(2,1)S(1)} %convolution_convert_fusion) | copy-start | bytes 196612
  72.9 74.1 %copy-start.1 = (bf16[128,512]{1,0:T(8,128)(2,1)S(1)}, bf16[128,512]{1,0:T(8,128)(2,1)}, u32[]{:S(2)}) copy-start(bf16[128,512]{1,0:T(8,128)(2,1)} %param.14) | copy-start | bytes 393220
  219.8 4.8 copy-start.3
  224.9 175.9 %copy-start.4 = (s32[256]{0:T(256)S(1)}, s32[256]{0:T(256)}, u32[]{:S(2)}) copy-start(s32[256]{0:T(256)} %param.15) | copy-start | bytes 3076
  400.7 8.9 %copy-start.5 = (f32[256]{0:T(256)}, f32[256]{0:T(256)S(1)}, u32[]{:S(2)}) copy-start(f32[256]{0:T(256)S(1)} %get-tuple-element.4) | copy-start | bytes 3076
  405.6 144.0 %reduce-scatter.3.cloned.1.call-start = ((), (), s32[]{:S(2)}) async-start(), calls=%async_computation.7 | async-start | bytes 2785280 | tf_op jit(solution)/shard_map/reduce_scatter | solution.py:87
Sparse Core Ops, SparseCore 0:
  10.7 59.7 all-gather.5
  72.3 69.8 all-gather.7
  143.9 75.7 all-gather.9
  222.3 60.2 all-gather.11
  284.3 69.8 all-gather.13
  405.7 50.5 reduce-scatter.4
  461.8 87.7 reduce-scatter.2
where the time goes:
time: 557 us; the launch traced here: 556 us
  waiting for transfers between devices  465 us (83%)
  blocking collectives  40.8 us (7%)
  matrix products  31.6 us (6%)
  between operations  14.3 us (3%)
    reduce_scatter x1, waiting for transfers between devices, on_device(): lax.psum_scatter(terms.astype(jnp.bfloat16), 'tensor', scatter_dimension=...  92 us
    all_gather x1, waiting for transfers between devices, on_device(): lax.all_gather(up_weight, 'dp', axis=0, tiled=True)  72.5 us
    all_gather x1, waiting for transfers between devices, on_device(): lax.all_gather(down_weight, 'dp', axis=0, tiled=True)  71.5 us
    all_gather x1, waiting for transfers between devices, on_device(): lax.all_gather(gate_weight, 'dp', axis=0, tiled=True)  69.2 us
    all_gather x1, waiting for transfers between devices, on_device(): lax.all_gather(tokens, 'tensor', axis=1, tiled=True)  59.2 us
    all_gather x1, waiting for transfers between devices, on_device(): lax.all_gather(upstream, 'tensor', axis=1, tiled=True)  57.7 us
    psum x1, blocking collectives, on_device(): log_ratio = lax.psum(partial_ratio, 'tensor') / math.sqrt(width)  40.8 us
    reduce_scatter x1, waiting for transfers between devices, on_device(): lax.psum_scatter(gradient_pieces.astype(jnp.bfloat16), 'dp', scatter_dime...  40.1 us
  transfers between devices with their start and end apart: 7, of which 7 were waited for; matrix products, arithmetic and copies ran while one was open for 5% of the time, Pallas kernels for 0%

commit v1 on v0

v1 whole, which is shorter than its diff:
```python
import math

import jax
import jax.numpy as jnp
from jax import lax
from jax.experimental import pallas as pl
from jax.experimental.pallas import tpu as pltpu
from jax.sharding import PartitionSpec as P

MESH = pl.DeviceIdType.MESH
BF16 = jnp.bfloat16
F32 = jnp.float32

adapter_scale = 0.5
beta_coef = 0.5
loss_scale = 128.0

ROWS = 256
BLK = 320
COLS = 256
RANK = 64
D = 5120


def nt(left, right):
    return lax.dot_general(left, right, (((1,), (1,)), ((), ())), preferred_element_type=F32)


def dot(left, right):
    return jnp.dot(left, right, preferred_element_type=F32)


def m4(v):
    return lax.rem(v + 4, 4)


def m8(v):
    return lax.rem(v + 8, 8)


def kernel(
    tok, ups, wg, wu, wd, aa_in, ab_in, mem,
    lr_out, ig_out, abg_out,
    xb, wb, aa, ab, mb, gu, rr, lw, hc, sb, rb, pb,
    r1, r2, r3, r4, lr_own, lr_sib, lr_one, lrx, lry, cf, apart, azb, afin, abr,
    xr, xd, xs, xds, xl, w0r, w0s, zr, zs, aas, abs_, mrs, d2s, d2r, rsr, rss, lrr, lrs, azr, azs, afr, afs,
):
    dp = lax.axis_index("dp")
    tp = lax.axis_index("tensor")
    yl, z = lax.div(dp, 8), lax.rem(dp, 8)
    x, yh, c = lax.div(tp, 4), lax.rem(lax.div(tp, 2), 2), lax.rem(tp, 2)
    y = yh * 2 + yl

    def dev(x_, y_, z_, c_):
        return {"dp": lax.rem(y_, 2) * 8 + z_, "tensor": x_ * 4 + lax.div(y_, 2) * 2 + c_}

    def copy(src, dst, ssem, rsem, to):
        return pltpu.make_async_remote_copy(
            src_ref=src, dst_ref=dst, send_sem=ssem, recv_sem=rsem, device_id=to, device_id_type=MESH
        )

    sib = dev(x, y, z, 1 - c)
    other_y = yh * 2 + (1 - yl)
    pending = []

    def send(*args):
        descriptor = copy(*args)
        descriptor.start()
        pending.append(descriptor)

    def got(dst, rsem):
        copy(dst, dst, rsem, rsem, sib).wait_recv()

    barrier = pltpu.get_barrier_semaphore()
    partners = [sib, dev(x, other_y, z, 1 - c)]
    partners += [dev(m4(x + i), y, z, c) for i in (1, 2, 3)]
    partners += [dev(x, m4(y + i), z, c) for i in (1, 2, 3)]
    partners += [dev(x, y, m8(z + i), c) for i in range(1, 8)]
    for partner in partners:
        pl.semaphore_signal(barrier, inc=1, device_id=partner, device_id_type=MESH)
    pl.semaphore_wait(barrier, len(partners))

    kf, ks = yl * 8 + z, (1 - yl) * 8 + z
    home = c == yl
    mats = (wg, wu, wd)

    def w0(b, m):
        return mats[m].at[:, b * COLS:(b + 1) * COLS], wb.at[kf, :, m * COLS:(m + 1) * COLS]

    def w0_local(b, m):
        return pltpu.make_async_copy(*w0(b, m), w0r.at[0, m])

    def w0_near(b, m):
        return copy(*w0(b, m), w0s.at[b, m], w0r.at[0, m], sib)

    def w0_far(b, m):
        return copy(*w0(b, m), w0s.at[b, m], w0r.at[1, m], dev(x, yh * 2 + c, z, b))

    def ab_local(b):
        return pltpu.make_async_copy(ab_in.at[:, b * COLS:(b + 1) * COLS], ab, abs_.at[0])

    def ab_near(b):
        return copy(ab_in.at[:, b * COLS:(b + 1) * COLS], ab, abs_.at[1], abs_.at[0], sib)

    for b in (0, 1):
        @pl.when(home & (c == b))
        def _():
            for m in range(3):
                w0_local(b, m).start()

        @pl.when(home & (c != b))
        def _():
            for m in range(3):
                w0_near(b, m).start()

    sources = (tok, ups)

    def place(t, i, j):
        return (m4(x + i), m4(y + j)) if t == 0 else (m4(x + j), m4(y + i))

    def slot(t, i, j, rows=slice(0, ROWS), core=None):
        px, py = place(t, i, j)
        return xb.at[t, c if core is None else core, px, py, rows]

    def to(t, i, j):
        px, py = place(t, i, j)
        return dev(px, py, z, c)

    halves = (slice(0, ROWS // 2), slice(ROWS // 2, ROWS))
    counts = [0, 0]

    def xsend(t, src, dst, i, j, key):
        n = counts[t]
        counts[t] += 1
        send(src, dst, xs.at[t, n], xr.at[(t,) + key], to(t, i, j))

    def share(t, i, j, src=None):
        send(slot(t, i, j) if src is None else src, slot(t, i, j), xds.at[t, i, j], xd.at[t, i, j], sib)

    own_local = [pltpu.make_async_copy(sources[t], slot(t, 0, 0), xl.at[t]) for t in (0, 1)]
    for t in (0, 1):
        own_local[t].start()
    for t in (0, 1):
        xsend(t, sources[t], slot(t, 0, 0), 1, 0, (3, 0, 0))
        xsend(t, sources[t], slot(t, 0, 0), -1, 0, (1, 0, 0))

    for b in (0, 1):
        @pl.when(jnp.logical_not(home))
        def _():
            for m in range(3):
                w0_far(b, m).start()

        @pl.when(home & (c == b))
        def _():
            ab_local(b).start()

        @pl.when(home & (c != b))
        def _():
            ab_near(b).start()

    aa_copy = pltpu.make_async_copy(aa_in, aa, aas.at[0])
    aa_copy.start()
    send(mem, mb.at[yl], mrs.at[0], mrs.at[1], dev(x, other_y, z, c))
    mb[yl] = mem[...]

    def w0_wait(first, k):
        for m in range(3):
            ref = wb.at[k, :, m * COLS:(m + 1) * COLS]
            if first:
                @pl.when(home)
                def _():
                    pltpu.make_async_copy(ref, ref, w0r.at[0, m]).wait()

                @pl.when(jnp.logical_not(home))
                def _():
                    got(ref, w0r.at[0, m])
            else:
                got(ref, w0r.at[1, m])

    up_z, down_z = dev(x, y, m8(z + 1), c), dev(x, y, m8(z - 1), c)

    w0_wait(True, kf)
    send(wb.at[kf], wb.at[kf], zs.at[0, 0], zr.at[2], up_z)
    send(wb.at[kf], wb.at[kf], zs.at[1, 0], zr.at[3], down_z)

    for t in (0, 1):
        xsend(t, sources[t], slot(t, 0, 0), 0, 1, (0, 3, 0))
        xsend(t, sources[t], slot(t, 0, 0), 0, -1, (0, 1, 0))
        share(t, 0, 0, sources[t])

    def across(t, i):
        xsend(t, slot(t, i, 0), slot(t, i, 0), 0, 1, (i % 4, 3, 0))
        xsend(t, slot(t, i, 0), slot(t, i, 0), 0, -1, (i % 4, 1, 0))
        share(t, i, 0)

    for t in (0, 1):
        for i, step, half in ((3, 1, 0), (1, -1, 1)):
            got(slot(t, i, 0), xr.at[t, i, 0, 0])
            xsend(t, slot(t, i, 0, halves[half]), slot(t, i, 0, halves[half]), step, 0, (2, 0, half))
    for t in (0, 1):
        across(t, 3)
        across(t, 1)

    w0_wait(False, ks)
    send(wb.at[ks], wb.at[ks], zs.at[0, 1], zr.at[4], up_z)
    send(wb.at[ks], wb.at[ks], zs.at[1, 1], zr.at[5], down_z)

    for t in (0, 1):
        for half in (0, 1):
            got(slot(t, 2, 0, halves[half]), xr.at[t, 2, 0, half])
        across(t, 2)

    def block_of(i):
        j = i - 2
        distance = lax.div(j, 4) + 1
        kind = lax.rem(j, 4)
        down = lax.rem(kind, 2)
        second = jnp.where(i == 15, 1, lax.div(kind, 2))
        zz = m8(z + jnp.where(down == 1, distance, -distance))
        zz = jnp.where(i < 2, z, zz)
        second = jnp.where(i < 2, i, second)
        return jnp.where(second == 1, 1 - yl, yl) * 8 + zz

    def zcopy(i, down, later):
        k = block_of(jnp.int32(i))
        return copy(wb.at[k], wb.at[k], zs.at[down, i], zr.at[later], down_z if down else up_z)

    def zstep(i):
        got(wb.at[block_of(jnp.int32(i))], zr.at[i])
        down = (i - 2) % 2
        later = i + 4 if i <= 10 else 15
        if i <= 10 or i == 13:
            send(*[wb.at[block_of(jnp.int32(i))]] * 2, zs.at[down, i], zr.at[later], down_z if down else up_z)

    for i in (2, 3):
        zstep(i)

    def pass_on(t, i):
        got(slot(t, i, 3), xr.at[t, i, 3, 0])
        xsend(t, slot(t, i, 3, halves[0]), slot(t, i, 3, halves[0]), 0, 1, (i, 2, 0))
        share(t, i, 3)
        got(slot(t, i, 1), xr.at[t, i, 1, 0])
        xsend(t, slot(t, i, 1, halves[1]), slot(t, i, 1, halves[1]), 0, -1, (i, 2, 1))
        share(t, i, 1)

    for i in (0, 3, 1):
        for t in (0, 1):
            pass_on(t, i)
    for i in (4, 5):
        zstep(i)
    for t in (0, 1):
        pass_on(t, 2)
    for i in (6, 7):
        zstep(i)
    for i in (0, 3, 1, 2):
        for t in (0, 1):
            for half in (0, 1):
                got(slot(t, i, 2, halves[half]), xr.at[t, i, 2, half])
            share(t, i, 2)
    for t in (0, 1):
        own_local[t].wait()
        for i in range(4):
            for j in range(4):
                got(slot(t, i, j, core=1 - c), xd.at[t, i, j])
    aa_copy.wait()

    gu[...] = jnp.zeros_like(gu)
    rr[...] = jnp.zeros_like(rr)
    lw[...] = jnp.zeros_like(lw)

    def forward(i, carry):
        for e in range(8, 16):
            @pl.when(i == e)
            def _():
                got(wb.at[block_of(jnp.int32(e))], zr.at[e])
                if e <= 10 or e == 13:
                    zcopy(e, (e - 2) % 2, e + 4 if e <= 10 else 15).start()

        k = block_of(i)
        kx, ky, kc = lax.div(k, 4), lax.rem(lax.div(k, 2), 2) * 2, lax.rem(k, 2)
        t = xb[0, kc, kx, pl.ds(ky, 2)].reshape(2 * ROWS, BLK)
        u = xb[1, kc, kx, pl.ds(ky, 2)].reshape(2 * ROWS, BLK)
        gu[...] += dot(t, wb[k, :, 0:2 * COLS])
        rr[...] += dot(u, wb[k, :, 2 * COLS:3 * COLS])
        lw[...] += dot(t, aa[k])
        return carry

    lax.fori_loop(0, 16, forward, 0)

    @pl.when(home)
    def _():
        pltpu.make_async_copy(ab, ab, abs_.at[0]).wait()

    @pl.when(jnp.logical_not(home))
    def _():
        got(ab, abs_.at[0])

    step = 128
    eye = lax.broadcasted_iota(jnp.int32, (step, step), 0) == lax.broadcasted_iota(jnp.int32, (step, step), 1)
    for r in range(2 * ROWS // step):
        rows = slice(r * step, (r + 1) * step)
        b_g, b_u = ab[0:RANK], ab[RANK:2 * RANK]
        gate, up, readout = gu[rows, 0:COLS], gu[rows, COLS:2 * COLS], rr[rows]
        low = lw[rows].astype(BF16)
        pol_gate = gate + adapter_scale * dot(low[:, 0:RANK], b_g)
        pol_up = up + adapter_scale * dot(low[:, RANK:2 * RANK], b_u)
        sig = jax.nn.sigmoid(pol_gate)
        act = pol_gate * sig
        shift = act * pol_up - gate * jax.nn.sigmoid(gate) * up
        part = jnp.sum(shift * readout, axis=1, keepdims=True)
        lr_own[:, rows] = jnp.sum(jnp.where(eye, part, 0.0), axis=0, keepdims=True)
        scaled = readout * (1.0 / math.sqrt(D))
        h_gate = (scaled * pol_up * (sig * (1.0 + pol_gate * (1.0 - sig)))).astype(BF16)
        h_up = (scaled * act).astype(BF16)
        hc[rows, 0:COLS] = h_gate
        hc[rows, COLS:2 * COLS] = h_up
        hc[rows, 2 * COLS:2 * COLS + RANK] = (adapter_scale * nt(h_gate, b_g)).astype(BF16)
        hc[rows, 2 * COLS + RANK:2 * COLS + 2 * RANK] = (adapter_scale * nt(h_up, b_u)).astype(BF16)

    send(lr_own, lr_sib, lrs.at[0], lrr.at[0], sib)

    def product(j, core):
        k = j * 2 + core
        return nt(hc[:, 0:2 * COLS], wb[k, :, 0:2 * COLS]) + nt(hc[:, 2 * COLS:], aa[k])

    def to_sib(j):
        return copy(sb.at[j], rb.at[j], d2s.at[j], d2r.at[j], sib)

    def back_send(j, carry):
        sb[j] = product(j, 1 - c).astype(BF16).reshape(2, ROWS, BLK)
        to_sib(j).start()
        return carry

    lax.fori_loop(0, 8, back_send, 0)

    got(lr_sib, lrr.at[0])
    lr_one[...] = lr_own[...] + lr_sib[...]
    lrx[x] = lr_one[...]
    for i in (1, 2, 3):
        send(lr_one, lrx.at[x], lrs.at[i], lrr.at[i], dev(m4(x + i), y, z, c))

    def back_own(j, carry):
        total = product(j, c).reshape(2, ROWS, BLK)
        to_sib(j).wait_recv()
        pb[lax.div(j, 2), pl.ds(lax.rem(j, 2) * 2, 2)] = (total + rb[j].astype(F32)).astype(BF16)
        return carry

    lax.fori_loop(0, 8, back_own, 0)

    def piece(h, i, q, rows):
        p = m4((x if h == 0 else y) + i)
        return (p, q, rows) if h == 0 else (q, p, rows)

    def hop(h, i):
        return dev(m4(x + i), y, z, c) if h == 0 else dev(x, m4(y + i), z, c)

    low_q, high_q, all_q = slice(0, 2), slice(2, 4), slice(0, 4)
    part_rows = (slice(0, 128), slice(128, 256))
    quarter = ((slice(0, 64), slice(64, 128)), (slice(128, 192), slice(192, 256)))

    def ring(stage, h, d, src, dst, target):
        send(src, dst, rss.at[h, stage, d], rsr.at[h, stage, d], target)

    def fold(idx, ref):
        pb[idx] = (pb[idx].astype(F32) + ref[...].astype(F32)).astype(BF16)

    for h in (0, 1):
        for d, q in ((0, low_q), (1, high_q)):
            ring(0, h, d, pb.at[piece(h, 2, q, part_rows[h])], r1.at[h, d], hop(h, 1 - 2 * d))

    for i in (1, 2, 3):
        got(lrx.at[m4(x - i)], lrr.at[i])
    lr_two = ((lrx[0] + lrx[1]) + lrx[2]) + lrx[3]
    lry[y] = lr_two
    for i in (1, 2, 3):
        send(lry.at[y], lry.at[y], lrs.at[3 + i], lrr.at[3 + i], dev(x, m4(y + i), z, c))

    for h in (0, 1):
        for d, q in ((0, low_q), (1, high_q)):
            got(r1.at[h, d], rsr.at[h, 0, d])
            side = 1 - 2 * d
            fold(piece(h, side, q, part_rows[h]), r1.at[h, d])
            ring(1, h, d, pb.at[piece(h, side, all_q, part_rows[h])], r2.at[h, d], hop(h, side))

    for i in (1, 2, 3):
        got(lry.at[m4(y - i)], lrr.at[3 + i])
    lr_row = (((lry[0] + lry[1]) + lry[2]) + lry[3]) / math.sqrt(D)
    got(mb.at[1 - yl], mrs.at[1])
    eye2 = lax.broadcasted_iota(jnp.int32, (ROWS, ROWS), 0) == lax.broadcasted_iota(jnp.int32, (ROWS, ROWS), 1)

    def column(row):
        return jnp.sum(jnp.where(eye2, row, 0.0), axis=1, keepdims=True)

    for g in (0, 1):
        members = mb[g]
        pair = lax.shift_right_logical(members, 1)
        side_row = (1 - 2 * (members - 2 * pair)).astype(F32)
        pair_row = pair.astype(F32)
        lr_g = lr_row[:, g * ROWS:(g + 1) * ROWS]
        value = side_row * (jnp.exp(lr_g) + lr_g)
        same = column(pair_row) == pair_row
        margin = beta_coef * jnp.sum(jnp.where(same, value, 0.0), axis=1, keepdims=True)
        weight = -loss_scale * beta_coef * jax.nn.sigmoid(-margin)
        cf[g] = weight * column(side_row) * (jnp.exp(column(lr_g)) + 1.0)

        @pl.when(yl == g)
        def _():
            lr_out[...] = lr_g

    coeff = cf[...].reshape(2 * ROWS, 1)
    low_t = (lw[...].astype(BF16).astype(F32) * coeff).T.astype(BF16)
    g_part = adapter_scale * dot(low_t[0:RANK], hc[:, 0:COLS])
    u_part = adapter_scale * dot(low_t[RANK:2 * RANK], hc[:, COLS:2 * COLS])
    apart[:, 0] = g_part.reshape(8, 8, COLS)
    apart[:, 1] = u_part.reshape(8, 8, COLS)
    for i in range(1, 8):
        send(apart.at[m8(z + i)], azb.at[z], azs.at[i], azr.at[i], dev(x, y, m8(z + i), c))
    azb[z] = apart[z]

    for h in (0, 1):
        for d in (0, 1):
            got(r2.at[h, d], rsr.at[h, 1, d])
        idx = piece(h, 0, all_q, part_rows[h])
        pb[idx] = (pb[idx].astype(F32) + r2[h, 0].astype(F32) + r2[h, 1].astype(F32)).astype(BF16)

    def last(h, j, rows):
        return (x, m4(y + j), rows) if h == 0 else (m4(x + j), y, rows)

    for h in (0, 1):
        for d in (0, 1):
            ring(2, h, d, pb.at[last(h, 2, quarter[h][d])], r3.at[h, d], hop(1 - h, 1 - 2 * d))

    for i in range(1, 8):
        got(azb.at[m8(z - i)], azr.at[i])
    total = azb[0]
    for i in range(1, 8):
        total = total + azb[i]
    afin[...] = total

    def a_near():
        return copy(afin.at[yl], abr.at[c], afs.at[0], afr.at[c], sib)

    def a_far():
        return copy(afin.at[1 - yl], abr.at[c], afs.at[1], afr.at[c], dev(x, other_y, z, yl))

    a_far().start()

    @pl.when(home)
    def _():
        abr[c] = afin[yl]

    @pl.when(jnp.logical_not(home))
    def _():
        a_near().start()

    for h in (0, 1):
        for d in (0, 1):
            got(r3.at[h, d], rsr.at[h, 2, d])
            side = 1 - 2 * d
            fold(last(h, side, quarter[h][d]), r3.at[h, d])
            ring(3, h, d, pb.at[last(h, side, part_rows[h])], r4.at[h, d], hop(1 - h, side))

    for h in (0, 1):
        for d in (0, 1):
            got(r4.at[h, d], rsr.at[h, 3, d])
        rows = part_rows[h]
        grad = pb[x, y, rows].astype(F32) + r4[h, 0].astype(F32) + r4[h, 1].astype(F32)
        ig_out[rows, :] = (grad * cf[yl, rows]).astype(BF16)

    @pl.when(home)
    def _():
        got(abr.at[1 - c], afr.at[1 - c])

    @pl.when(jnp.logical_not(home))
    def _():
        got(abr.at[0], afr.at[0])
        got(abr.at[1], afr.at[1])

    abg_out[:, 0:COLS] = abr[0]
    abg_out[:, COLS:2 * COLS] = abr[1]

    for descriptor in pending:
        descriptor.wait_send()
    for e in (8, 9, 10, 13):
        zcopy(e, (e - 2) % 2, e + 4 if e <= 10 else 15).wait_send()

    def sent(j, carry):
        to_sib(j).wait_send()
        return carry

    lax.fori_loop(0, 8, sent, 0)
    a_far().wait_send()

    @pl.when(jnp.logical_not(home))
    def _():
        a_near().wait_send()

    for b in (0, 1):
        @pl.when(home & (c != b))
        def _():
            for m in range(3):
                w0_near(b, m).wait_send()
            ab_near(b).wait_send()

        @pl.when(jnp.logical_not(home))
        def _():
            for m in range(3):
                w0_far(b, m).wait_send()


def on_device(tokens, upstream, gate_weight, up_weight, down_weight, adapter_a, adapter_b, membership):
    vmem, dma = pltpu.VMEM, pltpu.SemaphoreType.DMA
    anywhere = pl.BlockSpec(memory_space=pl.ANY)
    inside = pl.BlockSpec(memory_space=pltpu.VMEM)
    log_ratio, input_grad, b_gradient = pl.pallas_call(
        kernel,
        out_shape=(
            jax.ShapeDtypeStruct((1, ROWS), F32),
            jax.ShapeDtypeStruct((ROWS, BLK), BF16),
            jax.ShapeDtypeStruct((8, 2 * COLS), F32),
        ),
        in_specs=[anywhere] * 7 + [inside],
        out_specs=(inside,) * 3,
        scratch_shapes=[
            vmem((2, 2, 4, 4, ROWS, BLK), BF16),
            vmem((16, BLK, 3 * COLS), BF16),
            vmem((16, BLK, 2 * RANK), BF16),
            vmem((2 * RANK, COLS), BF16),
            vmem((2, 1, ROWS), jnp.int32),
            vmem((2 * ROWS, 2 * COLS), F32),
            vmem((2 * ROWS, COLS), F32),
            vmem((2 * ROWS, 2 * RANK), F32),
            vmem((2 * ROWS, 2 * COLS + 2 * RANK), BF16),
            vmem((8, 2, ROWS, BLK), BF16),
            vmem((8, 2, ROWS, BLK), BF16),
            vmem((4, 4, ROWS, BLK), BF16),
            vmem((2, 2, 2, 128, BLK), BF16),
            vmem((2, 2, 4, 128, BLK), BF16),
            vmem((2, 2, 64, BLK), BF16),
            vmem((2, 2, 128, BLK), BF16),
            vmem((1, 2 * ROWS), F32),
            vmem((1, 2 * ROWS), F32),
            vmem((1, 2 * ROWS), F32),
            vmem((4, 1, 2 * ROWS), F32),
            vmem((4, 1, 2 * ROWS), F32),
            vmem((2, ROWS, 1), F32),
            vmem((8, 2, 8, COLS), F32),
            vmem((8, 2, 8, COLS), F32),
            vmem((2, 8, COLS), F32),
            vmem((2, 8, COLS), F32),
            dma((2, 4, 4, 2)),
            dma((2, 4, 4)),
            dma((2, 24)),
            dma((2, 4, 4)),
            dma((2,)),
            dma((2, 3)),
            dma((2, 3)),
            dma((16,)),
            dma((2, 16)),
            dma((1,)),
            dma((2,)),
            dma((2,)),
            dma((8,)),
            dma((8,)),
            dma((2, 4, 2)),
            dma((2, 4, 2)),
            dma((7,)),
            dma((7,)),
            dma((8,)),
            dma((8,)),
            dma((2,)),
            dma((2,)),
        ],
        compiler_params=pltpu.CompilerParams(
            collective_id=0, has_side_effects=True, vmem_limit_bytes=56 * 1024 * 1024
        ),
    )(
        tokens, upstream, gate_weight, up_weight, down_weight,
        adapter_a.reshape(16, BLK, 2 * RANK), adapter_b, membership.reshape(1, ROWS),
    )
    return log_ratio.reshape(ROWS), input_grad, b_gradient


def solution(mesh):
    placed = (
        P("dp", "tensor"),
        P("dp", "tensor"),
        P("dp", "tensor"),
        P("dp", "tensor"),
        P("dp", "tensor"),
        P(),
        P(None, "tensor"),
        P("dp"),
    )
    return jax.shard_map(
        on_device,
        mesh=mesh,
        in_specs=placed,
        out_specs=(P("dp"), P("dp", "tensor"), P("dp", "tensor")),
        check_vma=False,
    )
```

time: 557 us -> 142 us (0.25)
  waiting for transfers between devices: 465 us -> 0 us
  Pallas kernels: 0 us -> 133 us
  blocking collectives: 40.8 us -> 0 us
  matrix products: 31.6 us -> 0 us
  between operations: 14.3 us -> 0.64 us
  local copies, waits for them, and re-layouts: 0.04 us -> 7.72 us
    all_gather x5 -> x0, waiting for transfers between devices: 330 us -> none  [the longest x1 72.5 us: on_device(): lax.all_gather(up_weight, 'dp', axis=0, tiled=True)]
    pallas_call x0 -> x1, Pallas kernels: none -> 133 us  [on_device(): pl.pallas_call(kernel, out_shape=(jax.ShapeDtypeStruct((1, ROWS), F32), j...]
    reduce_scatter x2 -> x0, waiting for transfers between devices: 132 us -> none  [the longest x1 92 us: on_device(): lax.psum_scatter(terms.astype(jnp.bfloat16), 'tensor', scatter_dimension=...]
    psum x1 -> x0, blocking collectives: 40.8 us -> none  [on_device(): log_ratio = lax.psum(partial_ratio, 'tensor') / math.sqrt(width)]
    dot_general x15 -> x0, matrix products: 31.6 us -> none  [the longest x5 10.9 us: transposed_product(): lax.dot_general(left, right, (((1,), (1,)), ((), ())), preferred_element_...]
    unnamed x12 -> x5, local copies, waits for them, and re-layouts: 0.04 us -> 7.72 us
  transfers between devices with their start and end apart: 7 -> 0, of which waited for: 7 -> 0; matrix products, arithmetic and copies ran while one was open for 5% -> 0% of each run, Pallas kernels for 0% -> 0%
where the time goes in v1:
time: 142 us; the launch traced here: 141 us
  Pallas kernels  133 us (94%)
  local copies, waits for them, and re-layouts  7.72 us (5%)
    pallas_call x1, Pallas kernels, on_device(): pl.pallas_call(kernel, out_shape=(jax.ShapeDtypeStruct((1, ROWS), F32), j...  133 us
    unnamed x5, local copies, waits for them, and re-layouts  7.72 us

profile of v1, /device:TPU:1, one launch (start us, length us, event | category | flops | bytes accessed | tf_op | source)
XLA Modules:
  0.0 141.3 jit_solution(10083824560917530770)
XLA Ops:
  0.6 1.7 %copy.11.tok = bf16[256,320]{1,0:T(8,128)(2,1)} copy(bf16[256,320]{0,1:T(8,128)(2,1)} %param.8) | data formatting | bytes 327680 | tf_op args[0]
  2.4 1.7 %copy.12.ups = bf16[256,320]{1,0:T(8,128)(2,1)} copy(bf16[256,320]{0,1:T(8,128)(2,1)} %param.9) | data formatting | bytes 327680 | tf_op args[1]
  4.1 132.9 %shard_map.103 = (f32[1,256]{1,0:T(1,128)}, bf16[256,320]{1,0:T(8,128)(2,1)}, f32[8,512]{1,0:T(8,128)}) custom-call(bf16[256,320]{1,0:T(8,128)(2,1)} %copy.11.tok, bf16[256,320]{1,0:T(8,128)(2,1)} %copy.12.ups, bf16[320,512]{1,0:T(8,128)(2,1)} %wg.1, bf16[320,512]{1,0:T(8,128)(2,1)} %wu.1, bf16[320,512]{1,0:T(8,128)(2,1)} %wd.1, ...), custom_call_target="tpu_custom_call" | custom-call | tf_op jit(solution)/shard_map/pallas_call | solution.py:515
  137.0 1.7 %copy.13 = bf16[256,320]{0,1:T(8,128)(2,1)} copy(bf16[256,320]{1,0:T(8,128)(2,1)} %get-tuple-element.10) | data formatting | bytes 327680
  138.8 1.2 copy.16
  140.0 1.3 copy.17

commit v2 on v1

--- a/solution.py
+++ b/solution.py
@@ -19,7 +19,12 @@
 BLK = 320
 COLS = 256
 RANK = 64
+W = 2 * RANK
 D = 5120
+
+
+def tn(left, right):
+    return lax.dot_general(left, right, (((0,), (0,)), ((), ())), preferred_element_type=F32)
 
 
 def nt(left, right):
@@ -41,9 +46,9 @@
 def kernel(
     tok, ups, wg, wu, wd, aa_in, ab_in, mem,
     lr_out, ig_out, abg_out,
-    xb, wb, aa, ab, mb, gu, rr, lw, hc, sb, rb, pb,
-    r1, r2, r3, r4, lr_own, lr_sib, lr_one, lrx, lry, cf, apart, azb, afin, abr,
-    xr, xd, xs, xds, xl, w0r, w0s, zr, zs, aas, abs_, mrs, d2s, d2r, rsr, rss, lrr, lrs, azr, azs, afr, afs,
+    xb, wb, ab, mb, gu, rr, hc, sb, rb, pb,
+    r1, r2, r3, r4, r5, r6, lr_own, lr_sib, lr_one, lrx, lry, cf, apart, azb, afin, abr,
+    xr, xd, xs, xds, xl, w0r, w0s, zr, zs, aas, abs_, mrs, d2s, d2r, rar, ras, rbr, rbs, rcr, rcs, lrr, lrs, azr, azs, afr, afs,
 ):
     dp = lax.axis_index("dp")
     tp = lax.axis_index("tensor")
@@ -85,7 +90,7 @@
     mats = (wg, wu, wd)
 
     def w0(b, m):
-        return mats[m].at[:, b * COLS:(b + 1) * COLS], wb.at[kf, :, m * COLS:(m + 1) * COLS]
+        return mats[m].at[:, b * COLS:(b + 1) * COLS], wb.at[kf, :, W + m * COLS:W + (m + 1) * COLS]
 
     def w0_local(b, m):
         return pltpu.make_async_copy(*w0(b, m), w0r.at[0, m])
@@ -118,7 +123,7 @@
     def place(t, i, j):
         return (m4(x + i), m4(y + j)) if t == 0 else (m4(x + j), m4(y + i))
 
-    def slot(t, i, j, rows=slice(0, ROWS), core=None):
+    def slot(t, i, j, rows=slice(0, BLK), core=None):
         px, py = place(t, i, j)
         return xb.at[t, c if core is None else core, px, py, rows]
 
@@ -126,7 +131,7 @@
         px, py = place(t, i, j)
         return dev(px, py, z, c)
 
-    halves = (slice(0, ROWS // 2), slice(ROWS // 2, ROWS))
+    halves = (slice(0, BLK // 2), slice(BLK // 2, BLK))
     counts = [0, 0]
 
     def xsend(t, src, dst, i, j, key):
@@ -158,14 +163,17 @@
         def _():
             ab_near(b).start()
 
-    aa_copy = pltpu.make_async_copy(aa_in, aa, aas.at[0])
+    aa_copy = pltpu.make_async_copy(aa_in, wb.at[:, :, 0:W], aas.at[0])
     aa_copy.start()
     send(mem, mb.at[yl], mrs.at[0], mrs.at[1], dev(x, other_y, z, c))
     mb[yl] = mem[...]
 
+    def weights(ref, k):
+        return ref.at[k, :, W:W + 3 * COLS]
+
     def w0_wait(first, k):
         for m in range(3):
-            ref = wb.at[k, :, m * COLS:(m + 1) * COLS]
+            ref = wb.at[k, :, W + m * COLS:W + (m + 1) * COLS]
             if first:
                 @pl.when(home)
                 def _():
@@ -180,8 +188,8 @@
     up_z, down_z = dev(x, y, m8(z + 1), c), dev(x, y, m8(z - 1), c)
 
     w0_wait(True, kf)
-    send(wb.at[kf], wb.at[kf], zs.at[0, 0], zr.at[2], up_z)
-    send(wb.at[kf], wb.at[kf], zs.at[1, 0], zr.at[3], down_z)
+    send(weights(wb, kf), weights(wb, kf), zs.at[0, 0], zr.at[2], up_z)
+    send(weights(wb, kf), weights(wb, kf), zs.at[1, 0], zr.at[3], down_z)
 
     for t in (0, 1):
         xsend(t, sources[t], slot(t, 0, 0), 0, 1, (0, 3, 0))
@@ -202,8 +210,8 @@
         across(t, 1)
 
     w0_wait(False, ks)
-    send(wb.at[ks], wb.at[ks], zs.at[0, 1], zr.at[4], up_z)
-    send(wb.at[ks], wb.at[ks], zs.at[1, 1], zr.at[5], down_z)
+    send(weights(wb, ks), weights(wb, ks), zs.at[0, 1], zr.at[4], up_z)
+    send(weights(wb, ks), weights(wb, ks), zs.at[1, 1], zr.at[5], down_z)
 
     for t in (0, 1):
         for half in (0, 1):
@@ -223,14 +231,14 @@
 
     def zcopy(i, down, later):
         k = block_of(jnp.int32(i))
-        return copy(wb.at[k], wb.at[k], zs.at[down, i], zr.at[later], down_z if down else up_z)
+        return copy(weights(wb, k), weights(wb, k), zs.at[down, i], zr.at[later], down_z if down else up_z)
 
     def zstep(i):
-        got(wb.at[block_of(jnp.int32(i))], zr.at[i])
+        got(weights(wb, block_of(jnp.int32(i))), zr.at[i])
         down = (i - 2) % 2
         later = i + 4 if i <= 10 else 15
         if i <= 10 or i == 13:
-            send(*[wb.at[block_of(jnp.int32(i))]] * 2, zs.at[down, i], zr.at[later], down_z if down else up_z)
+            send(*[weights(wb, block_of(jnp.int32(i)))] * 2, zs.at[down, i], zr.at[later], down_z if down else up_z)
 
     for i in (2, 3):
         zstep(i)
@@ -266,23 +274,21 @@
 
     gu[...] = jnp.zeros_like(gu)
     rr[...] = jnp.zeros_like(rr)
-    lw[...] = jnp.zeros_like(lw)
 
     def forward(i, carry):
         for e in range(8, 16):
             @pl.when(i == e)
             def _():
-                got(wb.at[block_of(jnp.int32(e))], zr.at[e])
+                got(weights(wb, block_of(jnp.int32(e))), zr.at[e])
                 if e <= 10 or e == 13:
                     zcopy(e, (e - 2) % 2, e + 4 if e <= 10 else 15).start()
 
         k = block_of(i)
         kx, ky, kc = lax.div(k, 4), lax.rem(lax.div(k, 2), 2) * 2, lax.rem(k, 2)
-        t = xb[0, kc, kx, pl.ds(ky, 2)].reshape(2 * ROWS, BLK)
-        u = xb[1, kc, kx, pl.ds(ky, 2)].reshape(2 * ROWS, BLK)
-        gu[...] += dot(t, wb[k, :, 0:2 * COLS])
-        rr[...] += dot(u, wb[k, :, 2 * COLS:3 * COLS])
-        lw[...] += dot(t, aa[k])
+        t = jnp.concatenate([xb[0, kc, kx, ky], xb[0, kc, kx, ky + 1]], axis=1)
+        u = jnp.concatenate([xb[1, kc, kx, ky], xb[1, kc, kx, ky + 1]], axis=1)
+        gu[...] += tn(wb[k, :, 0:W + 2 * COLS], t)
+        rr[...] += tn(wb[k, :, W + 2 * COLS:W + 3 * COLS], u)
         return carry
 
     lax.fori_loop(0, 16, forward, 0)
@@ -295,92 +301,146 @@
     def _():
         got(ab, abs_.at[0])
 
-    step = 128
-    eye = lax.broadcasted_iota(jnp.int32, (step, step), 0) == lax.broadcasted_iota(jnp.int32, (step, step), 1)
-    for r in range(2 * ROWS // step):
-        rows = slice(r * step, (r + 1) * step)
-        b_g, b_u = ab[0:RANK], ab[RANK:2 * RANK]
-        gate, up, readout = gu[rows, 0:COLS], gu[rows, COLS:2 * COLS], rr[rows]
-        low = lw[rows].astype(BF16)
-        pol_gate = gate + adapter_scale * dot(low[:, 0:RANK], b_g)
-        pol_up = up + adapter_scale * dot(low[:, RANK:2 * RANK], b_u)
+    low = gu[0:W].astype(BF16)
+    b_t = ab[...].astype(F32).T.astype(BF16)
+    step = 64
+    ratio = jnp.zeros((1, 2 * ROWS), F32)
+    for r in range(COLS // step):
+        units = slice(r * step, (r + 1) * step)
+        g_at, u_at = W + r * step, W + COLS + r * step
+        gate, up, readout = gu[g_at:g_at + step], gu[u_at:u_at + step], rr[units]
+        pol_gate = gate + adapter_scale * dot(b_t[units, 0:RANK], low[0:RANK])
+        pol_up = up + adapter_scale * dot(b_t[units, RANK:W], low[RANK:W])
         sig = jax.nn.sigmoid(pol_gate)
         act = pol_gate * sig
         shift = act * pol_up - gate * jax.nn.sigmoid(gate) * up
-        part = jnp.sum(shift * readout, axis=1, keepdims=True)
-        lr_own[:, rows] = jnp.sum(jnp.where(eye, part, 0.0), axis=0, keepdims=True)
+        ratio += jnp.sum(shift * readout, axis=0, keepdims=True)
         scaled = readout * (1.0 / math.sqrt(D))
-        h_gate = (scaled * pol_up * (sig * (1.0 + pol_gate * (1.0 - sig)))).astype(BF16)
-        h_up = (scaled * act).astype(BF16)
-        hc[rows, 0:COLS] = h_gate
-        hc[rows, COLS:2 * COLS] = h_up
-        hc[rows, 2 * COLS:2 * COLS + RANK] = (adapter_scale * nt(h_gate, b_g)).astype(BF16)
-        hc[rows, 2 * COLS + RANK:2 * COLS + 2 * RANK] = (adapter_scale * nt(h_up, b_u)).astype(BF16)
-
+        hc[g_at:g_at + step] = (scaled * pol_up * (sig * (1.0 + pol_gate * (1.0 - sig)))).astype(BF16)
+        hc[u_at:u_at + step] = (scaled * act).astype(BF16)
+    lr_own[...] = ratio
     send(lr_own, lr_sib, lrs.at[0], lrr.at[0], sib)
+    hc[0:RANK] = (adapter_scale * dot(ab[0:RANK], hc[W:W + COLS])).astype(BF16)
+    hc[RANK:W] = (adapter_scale * dot(ab[RANK:W], hc[W + COLS:])).astype(BF16)
+
+    first, second = slice(0, BLK // 2), slice(BLK // 2, BLK)
+
+    def order(j):
+        turn = lax.rem(j + 1, 3)
+        dx = jnp.where(j < 2, 2, jnp.where(turn == 0, 1, jnp.where(turn == 1, 3, 0)))
+        dh = jnp.where(j < 2, 1 - j, jnp.where(j < 5, 1, 0))
+        return lax.rem(x + dx, 4), lax.rem(yh + dh, 2)
 
     def product(j, core):
-        k = j * 2 + core
-        return nt(hc[:, 0:2 * COLS], wb[k, :, 0:2 * COLS]) + nt(hc[:, 2 * COLS:], aa[k])
+        bx, bh = order(j)
+        return dot(wb[bx * 4 + bh * 2 + core, :, 0:W + 2 * COLS], hc[...])
 
     def to_sib(j):
         return copy(sb.at[j], rb.at[j], d2s.at[j], d2r.at[j], sib)
 
-    def back_send(j, carry):
-        sb[j] = product(j, 1 - c).astype(BF16).reshape(2, ROWS, BLK)
+    def back_send(j):
+        sb[j] = product(j, 1 - c).astype(BF16)
         to_sib(j).start()
-        return carry
-
-    lax.fori_loop(0, 8, back_send, 0)
-
-    got(lr_sib, lrr.at[0])
-    lr_one[...] = lr_own[...] + lr_sib[...]
-    lrx[x] = lr_one[...]
-    for i in (1, 2, 3):
-        send(lr_one, lrx.at[x], lrs.at[i], lrr.at[i], dev(m4(x + i), y, z, c))
-
-    def back_own(j, carry):
-        total = product(j, c).reshape(2, ROWS, BLK)
-        to_sib(j).wait_recv()
-        pb[lax.div(j, 2), pl.ds(lax.rem(j, 2) * 2, 2)] = (total + rb[j].astype(F32)).astype(BF16)
-        return carry
-
-    lax.fori_loop(0, 8, back_own, 0)
-
-    def piece(h, i, q, rows):
-        p = m4((x if h == 0 else y) + i)
-        return (p, q, rows) if h == 0 else (q, p, rows)
-
-    def hop(h, i):
-        return dev(m4(x + i), y, z, c) if h == 0 else dev(x, m4(y + i), z, c)
-
-    low_q, high_q, all_q = slice(0, 2), slice(2, 4), slice(0, 4)
-    part_rows = (slice(0, 128), slice(128, 256))
-    quarter = ((slice(0, 64), slice(64, 128)), (slice(128, 192), slice(192, 256)))
-
-    def ring(stage, h, d, src, dst, target):
-        send(src, dst, rss.at[h, stage, d], rsr.at[h, stage, d], target)
+
+    up_x, down_x = dev(m4(x + 1), y, z, c), dev(m4(x - 1), y, z, c)
+    up_y, down_y = dev(x, m4(y + 1), z, c), dev(x, m4(y - 1), z, c)
+    far, near = (1 - yh) * 2, yh * 2
+    pairs = (pl.ds(far, 2), pl.ds(near, 2))
 
     def fold(idx, ref):
         pb[idx] = (pb[idx].astype(F32) + ref[...].astype(F32)).astype(BF16)
 
-    for h in (0, 1):
-        for d, q in ((0, low_q), (1, high_q)):
-            ring(0, h, d, pb.at[piece(h, 2, q, part_rows[h])], r1.at[h, d], hop(h, 1 - 2 * d))
-
-    for i in (1, 2, 3):
-        got(lrx.at[m4(x - i)], lrr.at[i])
-    lr_two = ((lrx[0] + lrx[1]) + lrx[2]) + lrx[3]
-    lry[y] = lr_two
-    for i in (1, 2, 3):
-        send(lry.at[y], lry.at[y], lrs.at[3 + i], lrr.at[3 + i], dev(x, m4(y + i), z, c))
-
-    for h in (0, 1):
-        for d, q in ((0, low_q), (1, high_q)):
-            got(r1.at[h, d], rsr.at[h, 0, d])
-            side = 1 - 2 * d
-            fold(piece(h, side, q, part_rows[h]), r1.at[h, d])
-            ring(1, h, d, pb.at[piece(h, side, all_q, part_rows[h])], r2.at[h, d], hop(h, side))
+    def a1(d):
+        return copy(pb.at[m4(x + 2), pairs[d], first], r1.at[d], ras.at[0, d], rar.at[0, d], (up_x, down_x)[d])
+
+    def a2(d, n):
+        return copy(
+            pb.at[m4(x + 1 - 2 * d), pairs[n], first], r2.at[d, n], ras.at[1 + n, d], rar.at[1 + n, d], (up_x, down_x)[d]
+        )
+
+    def a_fold(d):
+        got(r1.at[d], rar.at[0, d])
+        fold((m4(x + 1 - 2 * d), pairs[d], first), r1.at[d])
+
+    def b_dir(dx):
+        return 0 if dx in (1, 2) else 1
+
+    def b1(dx):
+        d = b_dir(dx)
+        return copy(pb.at[m4(x + dx), m4(y + 2), second], r3.at[dx], rbs.at[0, dx], rbr.at[0, dx], (up_y, down_y)[d])
+
+    def b2(dx, d):
+        return copy(
+            pb.at[m4(x + dx), m4(y + 1 - 2 * d), second], r4.at[d, dx], rbs.at[1 + d, dx], rbr.at[1 + d, dx], (up_y, down_y)[d]
+        )
+
+    def b_fold(dx):
+        got(r3.at[dx], rbr.at[0, dx])
+        fold((m4(x + dx), m4(y + 1 - 2 * b_dir(dx)), second), r3.at[dx])
+
+    def b_both(dx):
+        b_fold(dx)
+        b2(dx, 0).start()
+        b2(dx, 1).start()
+
+    def after(j):
+        if j == 0:
+            a1(0).start()
+            b1(2).start()
+        elif j == 1:
+            a1(1).start()
+        elif j == 2:
+            b1(1).start()
+        elif j == 3:
+            b1(3).start()
+            a2(1, 0).start()
+            a_fold(0)
+            a2(0, 0).start()
+        elif j == 4:
+            b1(0).start()
+            b_both(2)
+        elif j == 5:
+            a2(0, 1).start()
+            b_both(1)
+        elif j == 6:
+            a_fold(1)
+            a2(1, 1).start()
+            b_both(3)
+        else:
+            b_both(0)
+
+    back_send(0)
+
+    def backward(j, carry):
+        @pl.when(j < 7)
+        def _():
+            back_send(j + 1)
+
+        total = product(j, c)
+        to_sib(j).wait_recv()
+        bx, bh = order(j)
+        total = (total + rb[j].astype(F32)).astype(BF16)
+        pb[bx, bh * 2] = total[:, 0:ROWS]
+        pb[bx, bh * 2 + 1] = total[:, ROWS:]
+        for e in range(8):
+            @pl.when(j == e)
+            def _():
+                after(e)
+                if e == 1:
+                    got(lr_sib, lrr.at[0])
+                    lr_one[...] = lr_own[...] + lr_sib[...]
+                    lrx[x] = lr_one[...]
+                    for i in (1, 2, 3):
+                        copy(lr_one, lrx.at[x], lrs.at[i], lrr.at[i], dev(m4(x + i), y, z, c)).start()
+                if e == 4:
+                    for i in (1, 2, 3):
+                        got(lrx.at[m4(x - i)], lrr.at[i])
+                    lry[y] = ((lrx[0] + lrx[1]) + lrx[2]) + lrx[3]
+                    for i in (1, 2, 3):
+                        copy(lry.at[y], lry.at[y], lrs.at[3 + i], lrr.at[3 + i], dev(x, m4(y + i), z, c)).start()
+        return carry
+
+    lax.fori_loop(0, 8, backward, 0)
 
     for i in (1, 2, 3):
         got(lry.at[m4(y - i)], lrr.at[3 + i])
@@ -394,41 +454,57 @@
     for g in (0, 1):
         members = mb[g]
         pair = lax.shift_right_logical(members, 1)
-        side_row = (1 - 2 * (members - 2 * pair)).astype(F32)
-        pair_row = pair.astype(F32)
+        side = (1 - 2 * (members - 2 * pair)).astype(F32)
+        pair = pair.astype(F32)
         lr_g = lr_row[:, g * ROWS:(g + 1) * ROWS]
-        value = side_row * (jnp.exp(lr_g) + lr_g)
-        same = column(pair_row) == pair_row
-        margin = beta_coef * jnp.sum(jnp.where(same, value, 0.0), axis=1, keepdims=True)
-        weight = -loss_scale * beta_coef * jax.nn.sigmoid(-margin)
-        cf[g] = weight * column(side_row) * (jnp.exp(column(lr_g)) + 1.0)
+        growth = jnp.exp(lr_g)
+        same = column(pair) == pair
+        margin = beta_coef * jnp.sum(jnp.where(same, column(side * (growth + lr_g)), 0.0), axis=0, keepdims=True)
+        cf[g] = -loss_scale * beta_coef * jax.nn.sigmoid(-margin) * side * (growth + 1.0)
 
         @pl.when(yl == g)
         def _():
             lr_out[...] = lr_g
 
-    coeff = cf[...].reshape(2 * ROWS, 1)
-    low_t = (lw[...].astype(BF16).astype(F32) * coeff).T.astype(BF16)
-    g_part = adapter_scale * dot(low_t[0:RANK], hc[:, 0:COLS])
-    u_part = adapter_scale * dot(low_t[RANK:2 * RANK], hc[:, COLS:2 * COLS])
+    low_t = (gu[0:W].astype(BF16).astype(F32) * jnp.concatenate([cf[0], cf[1]], axis=1)).astype(BF16)
+    g_part = adapter_scale * nt(low_t[0:RANK], hc[W:W + COLS])
+    u_part = adapter_scale * nt(low_t[RANK:W], hc[W + COLS:])
     apart[:, 0] = g_part.reshape(8, 8, COLS)
     apart[:, 1] = u_part.reshape(8, 8, COLS)
     for i in range(1, 8):
         send(apart.at[m8(z + i)], azb.at[z], azs.at[i], azr.at[i], dev(x, y, m8(z + i), c))
     azb[z] = apart[z]
 
-    for h in (0, 1):
+    quarter = ((slice(0, 80), slice(80, 160)), (slice(160, 240), slice(240, 320)))
+
+    def near_of(h, i):
+        return (x, m4(y + i)) if h == 0 else (m4(x + i), y)
+
+    ways = ((up_y, down_y), (up_x, down_x))
+
+    def c1(h, d):
+        return copy(pb.at[near_of(h, 2) + (quarter[h][d],)], r5.at[h, d], rcs.at[0, h, d], rcr.at[0, h, d], ways[h][d])
+
+    def c2(h, d):
+        rows = (first, second)[h]
+        return copy(pb.at[near_of(h, 1 - 2 * d) + (rows,)], r6.at[h, d], rcs.at[1, h, d], rcr.at[1, h, d], ways[h][d])
+
+    for n in (0, 1):
         for d in (0, 1):
-            got(r2.at[h, d], rsr.at[h, 1, d])
-        idx = piece(h, 0, all_q, part_rows[h])
-        pb[idx] = (pb[idx].astype(F32) + r2[h, 0].astype(F32) + r2[h, 1].astype(F32)).astype(BF16)
-
-    def last(h, j, rows):
-        return (x, m4(y + j), rows) if h == 0 else (m4(x + j), y, rows)
-
-    for h in (0, 1):
+            got(r2.at[d, n], rar.at[1 + n, d])
+        idx = (x, pairs[n], first)
+        pb[idx] = (pb[idx].astype(F32) + r2[0, n].astype(F32) + r2[1, n].astype(F32)).astype(BF16)
+        if n == 0:
+            for d in (0, 1):
+                c1(0, d).start()
+    for i in (2, 1, 3, 0):
         for d in (0, 1):
-            ring(2, h, d, pb.at[last(h, 2, quarter[h][d])], r3.at[h, d], hop(1 - h, 1 - 2 * d))
+            got(r4.at[d, i], rbr.at[1 + d, i])
+        idx = (m4(x + i), y, second)
+        pb[idx] = (pb[idx].astype(F32) + r4[0, i].astype(F32) + r4[1, i].astype(F32)).astype(BF16)
+        if i == 2:
+            for d in (0, 1):
+                c1(1, d).start()
 
     for i in range(1, 8):
         got(azb.at[m8(z - i)], azr.at[i])
@@ -455,17 +531,16 @@
 
     for h in (0, 1):
         for d in (0, 1):
-            got(r3.at[h, d], rsr.at[h, 2, d])
-            side = 1 - 2 * d
-            fold(last(h, side, quarter[h][d]), r3.at[h, d])
-            ring(3, h, d, pb.at[last(h, side, part_rows[h])], r4.at[h, d], hop(1 - h, side))
+            got(r5.at[h, d], rcr.at[0, h, d])
+            fold(near_of(h, 1 - 2 * d) + (quarter[h][d],), r5.at[h, d])
+            c2(h, d).start()
 
     for h in (0, 1):
         for d in (0, 1):
-            got(r4.at[h, d], rsr.at[h, 3, d])
-        rows = part_rows[h]
-        grad = pb[x, y, rows].astype(F32) + r4[h, 0].astype(F32) + r4[h, 1].astype(F32)
-        ig_out[rows, :] = (grad * cf[yl, rows]).astype(BF16)
+            got(r6.at[h, d], rcr.at[1, h, d])
+        rows = (first, second)[h]
+        grad = pb[x, y, rows].astype(F32) + r6[h, 0].astype(F32) + r6[h, 1].astype(F32)
+        ig_out[rows, :] = (grad * cf[yl]).astype(BF16)
 
     @pl.when(home)
     def _():
@@ -489,6 +564,20 @@
         return carry
 
     lax.fori_loop(0, 8, sent, 0)
+    for d in (0, 1):
+        a1(d).wait_send()
+        for n in (0, 1):
+            a2(d, n).wait_send()
+        for dx in range(4):
+            b2(dx, d).wait_send()
+        for h in (0, 1):
+            c1(h, d).wait_send()
+            c2(h, d).wait_send()
+    for dx in range(4):
+        b1(dx).wait_send()
+    for i in (1, 2, 3):
+        copy(lr_one, lrx.at[x], lrs.at[i], lrr.at[i], dev(m4(x + i), y, z, c)).wait_send()
+        copy(lry.at[y], lry.at[y], lrs.at[3 + i], lrr.at[3 + i], dev(x, m4(y + i), z, c)).wait_send()
     a_far().wait_send()
 
     @pl.when(jnp.logical_not(home))
@@ -516,34 +605,34 @@
         kernel,
         out_shape=(
             jax.ShapeDtypeStruct((1, ROWS), F32),
-            jax.ShapeDtypeStruct((ROWS, BLK), BF16),
+            jax.ShapeDtypeStruct((BLK, ROWS), BF16),
             jax.ShapeDtypeStruct((8, 2 * COLS), F32),
         ),
         in_specs=[anywhere] * 7 + [inside],
         out_specs=(inside,) * 3,
         scratch_shapes=[
-            vmem((2, 2, 4, 4, ROWS, BLK), BF16),
-            vmem((16, BLK, 3 * COLS), BF16),
-            vmem((16, BLK, 2 * RANK), BF16),
+            vmem((2, 2, 4, 4, BLK, ROWS), BF16),
+            vmem((16, BLK, W + 3 * COLS), BF16),
             vmem((2 * RANK, COLS), BF16),
             vmem((2, 1, ROWS), jnp.int32),
-            vmem((2 * ROWS, 2 * COLS), F32),
-            vmem((2 * ROWS, COLS), F32),
-            vmem((2 * ROWS, 2 * RANK), F32),
-            vmem((2 * ROWS, 2 * COLS + 2 * RANK), BF16),
-            vmem((8, 2, ROWS, BLK), BF16),
-            vmem((8, 2, ROWS, BLK), BF16),
-            vmem((4, 4, ROWS, BLK), BF16),
-            vmem((2, 2, 2, 128, BLK), BF16),
-            vmem((2, 2, 4, 128, BLK), BF16),
-            vmem((2, 2, 64, BLK), BF16),
-            vmem((2, 2, 128, BLK), BF16),
+            vmem((W + 2 * COLS, 2 * ROWS), F32),
+            vmem((COLS, 2 * ROWS), F32),
+            vmem((W + 2 * COLS, 2 * ROWS), BF16),
+            vmem((8, BLK, 2 * ROWS), BF16),
+            vmem((8, BLK, 2 * ROWS), BF16),
+            vmem((4, 4, BLK, ROWS), BF16),
+            vmem((2, 2, BLK // 2, ROWS), BF16),
+            vmem((2, 2, 2, BLK // 2, ROWS), BF16),
+            vmem((4, BLK // 2, ROWS), BF16),
+            vmem((2, 4, BLK // 2, ROWS), BF16),
+            vmem((2, 2, BLK // 4, ROWS), BF16),
+            vmem((2, 2, BLK // 2, ROWS), BF16),
             vmem((1, 2 * ROWS), F32),
             vmem((1, 2 * ROWS), F32),
             vmem((1, 2 * ROWS), F32),
             vmem((4, 1, 2 * ROWS), F32),
             vmem((4, 1, 2 * ROWS), F32),
-            vmem((2, ROWS, 1), F32),
+            vmem((2, 1, ROWS), F32),
             vmem((8, 2, 8, COLS), F32),
             vmem((8, 2, 8, COLS), F32),
             vmem((2, 8, COLS), F32),
@@ -562,8 +651,12 @@
             dma((2,)),
             dma((8,)),
             dma((8,)),
-            dma((2, 4, 2)),
-            dma((2, 4, 2)),
+            dma((3, 2)),
+            dma((3, 2)),
+            dma((3, 4)),
+            dma((3, 4)),
+            dma((2, 2, 2)),
+            dma((2, 2, 2)),
             dma((7,)),
             dma((7,)),
             dma((8,)),
@@ -575,10 +668,10 @@
             collective_id=0, has_side_effects=True, vmem_limit_bytes=56 * 1024 * 1024
         ),
     )(
-        tokens, upstream, gate_weight, up_weight, down_weight,
+        tokens.T, upstream.T, gate_weight, up_weight, down_weight,
         adapter_a.reshape(16, BLK, 2 * RANK), adapter_b, membership.reshape(1, ROWS),
     )
-    return log_ratio.reshape(ROWS), input_grad, b_gradient
+    return log_ratio.reshape(ROWS), input_grad.T, b_gradient
 
 
 def solution(mesh):

time: 142 us -> 128 us (0.901)
  Pallas kernels: 133 us -> 123 us
  local copies, waits for them, and re-layouts: 7.72 us -> 4.14 us
    pallas_call x1, Pallas kernels: 133 us -> 123 us  [on_device(): pl.pallas_call(kernel, out_shape=(jax.ShapeDtypeStruct((1, ROWS), F32), j...]
    unnamed x5 -> x3, local copies, waits for them, and re-layouts: 7.72 us -> 4.14 us
where the time goes in v2:
time: 128 us
  Pallas kernels  123 us (96%)
  local copies, waits for them, and re-layouts  4.14 us (3%)
    pallas_call x1, Pallas kernels, on_device(): pl.pallas_call(kernel, out_shape=(jax.ShapeDtypeStruct((1, ROWS), F32), j...  123 us
    unnamed x3, local copies, waits for them, and re-layouts  4.14 us

profile of v2, /device:TPU:1, one launch (start us, length us, event | category | flops | bytes accessed | tf_op | source)
XLA Modules:
  0.0 128.0 jit_solution(14892978273562287006)
XLA Ops:
  0.6 123.2 %shard_map.103 = (f32[1,256]{1,0:T(1,128)}, bf16[320,256]{1,0:T(8,128)(2,1)}, f32[8,512]{1,0:T(8,128)}) custom-call(bf16[320,256]{1,0:T(8,128)(2,1)} %bitcast.7, bf16[320,256]{1,0:T(8,128)(2,1)} %bitcast.8, bf16[320,512]{1,0:T(8,128)(2,1)} %wg.1, bf16[320,512]{1,0:T(8,128)(2,1)} %wu.1, bf16[320,512]{1,0:T(8,128)(2,1)} %wd.1, bf16[16,320,128]{2,1,0:T(8,128)(2,1)} %bitcast.6, ...), custom_call_target="tpu_custom_call" | custom-call | tf_op jit(solution)/shard_map/pallas_call | solution.py:604
  123.8 1.2 copy.14
  125.1 1.6 %copy.15 = bf16[256,320]{0,1:T(8,128)(2,1)} copy(bf16[256,320]{0,1:T(8,128)(2,1)} %bitcast.9) | data formatting | bytes 327680
  126.7 1.3 %copy.16 = f32[8,512]{1,0:T(8,128)} copy(f32[8,512]{1,0:T(8,128)} %get-tuple-element.14) | data formatting | bytes 32768

commit v3 on v2

--- a/solution.py
+++ b/solution.py
@@ -595,6 +595,12 @@
         def _():
             for m in range(3):
                 w0_far(b, m).wait_send()
+
+
+def hand_on(lr_in, ig_in, abg_in, lr_out, ig_out, abg_out):
+    lr_out[...] = lr_in[0]
+    ig_out[...] = ig_in[...]
+    abg_out[...] = abg_in[...]
 
 
 def on_device(tokens, upstream, gate_weight, up_weight, down_weight, adapter_a, adapter_b, membership):
@@ -671,7 +677,17 @@
         tokens.T, upstream.T, gate_weight, up_weight, down_weight,
         adapter_a.reshape(16, BLK, 2 * RANK), adapter_b, membership.reshape(1, ROWS),
     )
-    return log_ratio.reshape(ROWS), input_grad.T, b_gradient
+    log_ratio, input_grad, b_gradient = pl.pallas_call(
+        hand_on,
+        out_shape=(
+            jax.ShapeDtypeStruct((ROWS,), F32),
+            jax.ShapeDtypeStruct((BLK, ROWS), BF16),
+            jax.ShapeDtypeStruct((8, 2 * COLS), F32),
+        ),
+        in_specs=[inside] * 3,
+        out_specs=(inside,) * 3,
+    )(log_ratio, input_grad, b_gradient)
+    return log_ratio, input_grad.T, b_gradient
 
 
 def solution(mesh):

time: 128 us -> 126 us (0.984)
  local copies, waits for them, and re-layouts: 4.14 us -> 0 us
  Pallas kernels: 123 us -> 125 us
    unnamed x3 -> x0, local copies, waits for them, and re-layouts: 4.14 us -> none
    pallas_call x0 -> x1, Pallas kernels: none -> 1.6 us  [on_device(): pl.pallas_call(hand_on, out_shape=(jax.ShapeDtypeStruct((ROWS,), F32), ja...]
where the time goes in v3:
time: 126 us; the launch traced here: 125 us
  Pallas kernels  125 us (99%)
    pallas_call x1, Pallas kernels, on_device(): pl.pallas_call(kernel, out_shape=(jax.ShapeDtypeStruct((1, ROWS), F32), j...  123 us

profile of v3, /device:TPU:1, one launch (start us, length us, event | category | flops | bytes accessed | tf_op | source)
XLA Modules:
  0.0 125.4 jit_solution(14795446016773966237)
XLA Ops:
  0.6 123.2 %shard_map.103 = (f32[1,256]{1,0:T(1,128)}, bf16[320,256]{1,0:T(8,128)(2,1)}, f32[8,512]{1,0:T(8,128)}) custom-call(bf16[320,256]{1,0:T(8,128)(2,1)} %bitcast.6, bf16[320,256]{1,0:T(8,128)(2,1)} %bitcast.7, bf16[320,512]{1,0:T(8,128)(2,1)} %wg.1, bf16[320,512]{1,0:T(8,128)(2,1)} %wu.1, bf16[320,512]{1,0:T(8,128)(2,1)} %wd.1, bf16[16,320,128]{2,1,0:T(8,128)(2,1)} %bitcast.5, ...), custom_call_target="tpu_custom_call" | custom-call | tf_op jit(solution)/shard_map/pallas_call | solution.py:610
  123.8 1.6 %shard_map.104 = (f32[256]{0:T(256)}, bf16[320,256]{1,0:T(8,128)(2,1)}, f32[8,512]{1,0:T(8,128)}) custom-call(f32[1,256]{1,0:T(1,128)} %get-tuple-element.9.lr_in, bf16[320,256]{1,0:T(8,128)(2,1)} %get-tuple-element.10.ig_in, f32[8,512]{1,0:T(8,128)} %get-tuple-element.11.abg_in), custom_call_target="tpu_custom_call" | custom-call | tf_op jit(solution)/shard_map/pallas_call | solution.py:680

commit v4 on v3

--- a/solution.py
+++ b/solution.py
@@ -21,6 +21,7 @@
 RANK = 64
 W = 2 * RANK
 D = 5120
+CUT = 176
 
 
 def tn(left, right):
@@ -47,7 +48,7 @@
     tok, ups, wg, wu, wd, aa_in, ab_in, mem,
     lr_out, ig_out, abg_out,
     xb, wb, ab, mb, gu, rr, hc, sb, rb, pb,
-    r1, r2, r3, r4, r5, r6, lr_own, lr_sib, lr_one, lrx, lry, cf, apart, azb, afin, abr,
+    r1, r2, r3, r4, r5, r6, lr_own, lrx, lry, cf, apart, azb, afin, abr,
     xr, xd, xs, xds, xl, w0r, w0s, zr, zs, aas, abs_, mrs, d2s, d2r, rar, ras, rbr, rbs, rcr, rcs, lrr, lrs, azr, azs, afr, afs,
 ):
     dp = lax.axis_index("dp")
@@ -79,6 +80,7 @@
     barrier = pltpu.get_barrier_semaphore()
     partners = [sib, dev(x, other_y, z, 1 - c)]
     partners += [dev(m4(x + i), y, z, c) for i in (1, 2, 3)]
+    partners += [dev(m4(x + i), y, z, 1 - c) for i in (1, 2, 3)]
     partners += [dev(x, m4(y + i), z, c) for i in (1, 2, 3)]
     partners += [dev(x, y, m8(z + i), c) for i in range(1, 8)]
     for partner in partners:
@@ -319,11 +321,22 @@
         hc[g_at:g_at + step] = (scaled * pol_up * (sig * (1.0 + pol_gate * (1.0 - sig)))).astype(BF16)
         hc[u_at:u_at + step] = (scaled * act).astype(BF16)
     lr_own[...] = ratio
-    send(lr_own, lr_sib, lrs.at[0], lrr.at[0], sib)
+    lrx[x, c] = ratio
+    around = [(i, f) for i in range(4) for f in (0, 1) if i or f]
+
+    def lr_send(i, f):
+        n, core = 2 * i + f, 1 - c if f else c
+        return copy(lr_own, lrx.at[x, c], lrs.at[n], lrr.at[n], dev(m4(x + i), y, z, core))
+
+    def lr_send_y(i):
+        return copy(lry.at[y], lry.at[y], lrs.at[7 + i], lrr.at[7 + i], dev(x, m4(y + i), z, c))
+
+    for i, f in around:
+        lr_send(i, f).start()
     hc[0:RANK] = (adapter_scale * dot(ab[0:RANK], hc[W:W + COLS])).astype(BF16)
     hc[RANK:W] = (adapter_scale * dot(ab[RANK:W], hc[W + COLS:])).astype(BF16)
 
-    first, second = slice(0, BLK // 2), slice(BLK // 2, BLK)
+    first, second = slice(0, CUT), slice(CUT, BLK)
 
     def order(j):
         turn = lax.rem(j + 1, 3)
@@ -409,6 +422,75 @@
         else:
             b_both(0)
 
+    def az_send(i):
+        return copy(apart.at[m8(z + i)], azb.at[z], azs.at[i], azr.at[i], dev(x, y, m8(z + i), c))
+
+    def coefficients():
+        for i in (1, 2, 3):
+            got(lry.at[m4(y - i)], lrr.at[7 + i])
+        lr_row = (((lry[0] + lry[1]) + lry[2]) + lry[3]) / math.sqrt(D)
+        got(mb.at[1 - yl], mrs.at[1])
+        eye2 = lax.broadcasted_iota(jnp.int32, (ROWS, ROWS), 0) == lax.broadcasted_iota(jnp.int32, (ROWS, ROWS), 1)
+
+        def column(row):
+            return jnp.sum(jnp.where(eye2, row, 0.0), axis=1, keepdims=True)
+
+        for g in (0, 1):
+            members = mb[g]
+            pair = lax.shift_right_logical(members, 1)
+            side = (1 - 2 * (members - 2 * pair)).astype(F32)
+            pair = pair.astype(F32)
+            lr_g = lr_row[:, g * ROWS:(g + 1) * ROWS]
+            growth = jnp.exp(lr_g)
+            same = column(pair) == pair
+            margin = beta_coef * jnp.sum(jnp.where(same, column(side * (growth + lr_g)), 0.0), axis=0, keepdims=True)
+            cf[g] = -loss_scale * beta_coef * jax.nn.sigmoid(-margin) * side * (growth + 1.0)
+
+            @pl.when(yl == g)
+            def _():
+                lr_out[...] = lr_g
+
+        low_t = (gu[0:W].astype(BF16).astype(F32) * jnp.concatenate([cf[0], cf[1]], axis=1)).astype(BF16)
+        g_part = adapter_scale * nt(low_t[0:RANK], hc[W:W + COLS])
+        u_part = adapter_scale * nt(low_t[RANK:W], hc[W + COLS:])
+        apart[:, 0] = g_part.reshape(8, 8, COLS)
+        apart[:, 1] = u_part.reshape(8, 8, COLS)
+        for i in range(1, 8):
+            az_send(i).start()
+        azb[z] = apart[z]
+
+    def a_near():
+        return copy(afin.at[yl], abr.at[c], afs.at[0], afr.at[c], sib)
+
+    def a_far():
+        return copy(afin.at[1 - yl], abr.at[c], afs.at[1], afr.at[c], dev(x, other_y, z, yl))
+
+    def hand_out():
+        for i in range(1, 8):
+            got(azb.at[m8(z - i)], azr.at[i])
+        total = azb[0]
+        for i in range(1, 8):
+            total = total + azb[i]
+        afin[...] = total
+
+        a_far().start()
+
+        @pl.when(home)
+        def _():
+            abr[c] = afin[yl]
+
+        @pl.when(jnp.logical_not(home))
+        def _():
+            a_near().start()
+
+    def log_ratios():
+        for i, f in around:
+            got(lrx.at[m4(x - i), 1 - c if f else c], lrr.at[2 * i + f])
+        rows = [lrx[i, 0] + lrx[i, 1] for i in range(4)]
+        lry[y] = ((rows[0] + rows[1]) + rows[2]) + rows[3]
+        for i in (1, 2, 3):
+            lr_send_y(i).start()
+
     back_send(0)
 
     def backward(j, carry):
@@ -427,55 +509,16 @@
             def _():
                 after(e)
                 if e == 1:
-                    got(lr_sib, lrr.at[0])
-                    lr_one[...] = lr_own[...] + lr_sib[...]
-                    lrx[x] = lr_one[...]
-                    for i in (1, 2, 3):
-                        copy(lr_one, lrx.at[x], lrs.at[i], lrr.at[i], dev(m4(x + i), y, z, c)).start()
-                if e == 4:
-                    for i in (1, 2, 3):
-                        got(lrx.at[m4(x - i)], lrr.at[i])
-                    lry[y] = ((lrx[0] + lrx[1]) + lrx[2]) + lrx[3]
-                    for i in (1, 2, 3):
-                        copy(lry.at[y], lry.at[y], lrs.at[3 + i], lrr.at[3 + i], dev(x, m4(y + i), z, c)).start()
+                    log_ratios()
+                if e == 5:
+                    coefficients()
         return carry
 
     lax.fori_loop(0, 8, backward, 0)
 
-    for i in (1, 2, 3):
-        got(lry.at[m4(y - i)], lrr.at[3 + i])
-    lr_row = (((lry[0] + lry[1]) + lry[2]) + lry[3]) / math.sqrt(D)
-    got(mb.at[1 - yl], mrs.at[1])
-    eye2 = lax.broadcasted_iota(jnp.int32, (ROWS, ROWS), 0) == lax.broadcasted_iota(jnp.int32, (ROWS, ROWS), 1)
-
-    def column(row):
-        return jnp.sum(jnp.where(eye2, row, 0.0), axis=1, keepdims=True)
-
-    for g in (0, 1):
-        members = mb[g]
-        pair = lax.shift_right_logical(members, 1)
-        side = (1 - 2 * (members - 2 * pair)).astype(F32)
-        pair = pair.astype(F32)
-        lr_g = lr_row[:, g * ROWS:(g + 1) * ROWS]
-        growth = jnp.exp(lr_g)
-        same = column(pair) == pair
-        margin = beta_coef * jnp.sum(jnp.where(same, column(side * (growth + lr_g)), 0.0), axis=0, keepdims=True)
-        cf[g] = -loss_scale * beta_coef * jax.nn.sigmoid(-margin) * side * (growth + 1.0)
-
-        @pl.when(yl == g)
-        def _():
-            lr_out[...] = lr_g
-
-    low_t = (gu[0:W].astype(BF16).astype(F32) * jnp.concatenate([cf[0], cf[1]], axis=1)).astype(BF16)
-    g_part = adapter_scale * nt(low_t[0:RANK], hc[W:W + COLS])
-    u_part = adapter_scale * nt(low_t[RANK:W], hc[W + COLS:])
-    apart[:, 0] = g_part.reshape(8, 8, COLS)
-    apart[:, 1] = u_part.reshape(8, 8, COLS)
-    for i in range(1, 8):
-        send(apart.at[m8(z + i)], azb.at[z], azs.at[i], azr.at[i], dev(x, y, m8(z + i), c))
-    azb[z] = apart[z]
-
-    quarter = ((slice(0, 80), slice(80, 160)), (slice(160, 240), slice(240, 320)))
+    quarter = ((slice(0, 96), slice(96, CUT)), (slice(CUT, 256), slice(256, BLK)))
+    size = ((96, CUT - 96), (256 - CUT, BLK - 256))
+    span = (CUT, BLK - CUT)
 
     def near_of(h, i):
         return (x, m4(y + i)) if h == 0 else (m4(x + i), y)
@@ -483,63 +526,49 @@
     ways = ((up_y, down_y), (up_x, down_x))
 
     def c1(h, d):
-        return copy(pb.at[near_of(h, 2) + (quarter[h][d],)], r5.at[h, d], rcs.at[0, h, d], rcr.at[0, h, d], ways[h][d])
+        return copy(pb.at[near_of(h, 2) + (quarter[h][d],)], r5.at[h, d, 0:size[h][d]], rcs.at[0, h, d], rcr.at[0, h, d], ways[h][d])
 
     def c2(h, d):
         rows = (first, second)[h]
-        return copy(pb.at[near_of(h, 1 - 2 * d) + (rows,)], r6.at[h, d], rcs.at[1, h, d], rcr.at[1, h, d], ways[h][d])
-
-    for n in (0, 1):
+        return copy(pb.at[near_of(h, 1 - 2 * d) + (rows,)], r6.at[h, d, 0:span[h]], rcs.at[1, h, d], rcr.at[1, h, d], ways[h][d])
+
+    def x_sum(n):
         for d in (0, 1):
             got(r2.at[d, n], rar.at[1 + n, d])
         idx = (x, pairs[n], first)
         pb[idx] = (pb[idx].astype(F32) + r2[0, n].astype(F32) + r2[1, n].astype(F32)).astype(BF16)
-        if n == 0:
-            for d in (0, 1):
-                c1(0, d).start()
-    for i in (2, 1, 3, 0):
+
+    def y_sum(i):
         for d in (0, 1):
             got(r4.at[d, i], rbr.at[1 + d, i])
         idx = (m4(x + i), y, second)
         pb[idx] = (pb[idx].astype(F32) + r4[0, i].astype(F32) + r4[1, i].astype(F32)).astype(BF16)
-        if i == 2:
-            for d in (0, 1):
-                c1(1, d).start()
-
-    for i in range(1, 8):
-        got(azb.at[m8(z - i)], azr.at[i])
-    total = azb[0]
-    for i in range(1, 8):
-        total = total + azb[i]
-    afin[...] = total
-
-    def a_near():
-        return copy(afin.at[yl], abr.at[c], afs.at[0], afr.at[c], sib)
-
-    def a_far():
-        return copy(afin.at[1 - yl], abr.at[c], afs.at[1], afr.at[c], dev(x, other_y, z, yl))
-
-    a_far().start()
-
-    @pl.when(home)
-    def _():
-        abr[c] = afin[yl]
-
-    @pl.when(jnp.logical_not(home))
-    def _():
-        a_near().start()
+
+    def second_hop(h):
+        for d in (0, 1):
+            got(r5.at[h, d, 0:size[h][d]], rcr.at[0, h, d])
+            fold(near_of(h, 1 - 2 * d) + (quarter[h][d],), r5.at[h, d, 0:size[h][d]])
+            c2(h, d).start()
+
+    x_sum(0)
+    for d in (0, 1):
+        c1(0, d).start()
+    y_sum(2)
+    for d in (0, 1):
+        c1(1, d).start()
+    x_sum(1)
+    y_sum(1)
+    second_hop(0)
+    y_sum(3)
+    second_hop(1)
+    y_sum(0)
+    hand_out()
 
     for h in (0, 1):
         for d in (0, 1):
-            got(r5.at[h, d], rcr.at[0, h, d])
-            fold(near_of(h, 1 - 2 * d) + (quarter[h][d],), r5.at[h, d])
-            c2(h, d).start()
-
-    for h in (0, 1):
-        for d in (0, 1):
-            got(r6.at[h, d], rcr.at[1, h, d])
+            got(r6.at[h, d, 0:span[h]], rcr.at[1, h, d])
         rows = (first, second)[h]
-        grad = pb[x, y, rows].astype(F32) + r6[h, 0].astype(F32) + r6[h, 1].astype(F32)
+        grad = pb[x, y, rows].astype(F32) + r6[h, 0, 0:span[h]].astype(F32) + r6[h, 1, 0:span[h]].astype(F32)
         ig_out[rows, :] = (grad * cf[yl]).astype(BF16)
 
     @pl.when(home)
@@ -575,9 +604,12 @@
             c2(h, d).wait_send()
     for dx in range(4):
         b1(dx).wait_send()
+    for i, f in around:
+        lr_send(i, f).wait_send()
     for i in (1, 2, 3):
-        copy(lr_one, lrx.at[x], lrs.at[i], lrr.at[i], dev(m4(x + i), y, z, c)).wait_send()
-        copy(lry.at[y], lry.at[y], lrs.at[3 + i], lrr.at[3 + i], dev(x, m4(y + i), z, c)).wait_send()
+        lr_send_y(i).wait_send()
+    for i in range(1, 8):
+        az_send(i).wait_send()
     a_far().wait_send()
 
     @pl.when(jnp.logical_not(home))
@@ -627,16 +659,14 @@
             vmem((8, BLK, 2 * ROWS), BF16),
             vmem((8, BLK, 2 * ROWS), BF16),
             vmem((4, 4, BLK, ROWS), BF16),
-            vmem((2, 2, BLK // 2, ROWS), BF16),
-            vmem((2, 2, 2, BLK // 2, ROWS), BF16),
-            vmem((4, BLK // 2, ROWS), BF16),
-            vmem((2, 4, BLK // 2, ROWS), BF16),
-            vmem((2, 2, BLK // 4, ROWS), BF16),
-            vmem((2, 2, BLK // 2, ROWS), BF16),
+            vmem((2, 2, CUT, ROWS), BF16),
+            vmem((2, 2, 2, CUT, ROWS), BF16),
+            vmem((4, BLK - CUT, ROWS), BF16),
+            vmem((2, 4, BLK - CUT, ROWS), BF16),
+            vmem((2, 2, 96, ROWS), BF16),
+            vmem((2, 2, CUT, ROWS), BF16),
             vmem((1, 2 * ROWS), F32),
-            vmem((1, 2 * ROWS), F32),
-            vmem((1, 2 * ROWS), F32),
-            vmem((4, 1, 2 * ROWS), F32),
+            vmem((4, 2, 1, 2 * ROWS), F32),
             vmem((4, 1, 2 * ROWS), F32),
             vmem((2, 1, ROWS), F32),
             vmem((8, 2, 8, COLS), F32),
@@ -663,8 +693,8 @@
             dma((3, 4)),
             dma((2, 2, 2)),
             dma((2, 2, 2)),
-            dma((7,)),
-            dma((7,)),
+            dma((11,)),
+            dma((11,)),
             dma((8,)),
             dma((8,)),
             dma((2,)),

time: 126 us -> 125 us (level)
  no operation moved by 1% of the time
where the time goes in v4:
time: 125 us
  Pallas kernels  124 us (99%)
    pallas_call x1, Pallas kernels, on_device(): pl.pallas_call(kernel, out_shape=(jax.ShapeDtypeStruct((1, ROWS), F32), j...  122 us

profile of v4, /device:TPU:1, one launch (start us, length us, event | category | flops | bytes accessed | tf_op | source)
XLA Modules:
  0.0 124.6 jit_solution(2035076040485484180)
XLA Ops:
  0.6 122.4 %shard_map.103 = (f32[1,256]{1,0:T(1,128)}, bf16[320,256]{1,0:T(8,128)(2,1)}, f32[8,512]{1,0:T(8,128)}) custom-call(bf16[320,256]{1,0:T(8,128)(2,1)} %bitcast.6, bf16[320,256]{1,0:T(8,128)(2,1)} %bitcast.7, bf16[320,512]{1,0:T(8,128)(2,1)} %wg.1, bf16[320,512]{1,0:T(8,128)(2,1)} %wu.1, bf16[320,512]{1,0:T(8,128)(2,1)} %wd.1, bf16[16,320,128]{2,1,0:T(8,128)(2,1)} %bitcast.5, ...), custom_call_target="tpu_custom_call" | custom-call | tf_op jit(solution)/shard_map/pallas_call | solution.py:642
  123.0 1.6 %shard_map.104 = (f32[256]{0:T(256)}, bf16[320,256]{1,0:T(8,128)(2,1)}, f32[8,512]{1,0:T(8,128)}) custom-call(f32[1,256]{1,0:T(1,128)} %get-tuple-element.9.lr_in, bf16[320,256]{1,0:T(8,128)(2,1)} %get-tuple-element.10.ig_in, f32[8,512]{1,0:T(8,128)} %get-tuple-element.11.abg_in), custom_call_target="tpu_custom_call" | custom-call | tf_op jit(solution)/shard_map/pallas_call | solution.py:710

commit v5 on v4

--- a/solution.py
+++ b/solution.py
@@ -407,10 +407,10 @@
         elif j == 3:
             b1(3).start()
             a2(1, 0).start()
+        elif j == 4:
+            b1(0).start()
             a_fold(0)
             a2(0, 0).start()
-        elif j == 4:
-            b1(0).start()
             b_both(2)
         elif j == 5:
             a2(0, 1).start()

time: 125 us -> 124 us (level)
  no operation moved by 1% of the time
where the time goes in v5:
time: 124 us
  Pallas kernels  123 us (99%)
    pallas_call x1, Pallas kernels, on_device(): pl.pallas_call(kernel, out_shape=(jax.ShapeDtypeStruct((1, ROWS), F32), j...  122 us

profile of v5, /device:TPU:1, one launch (start us, length us, event | category | flops | bytes accessed | tf_op | source)
XLA Modules:
  0.0 123.9 jit_solution(13697134019418820727)
XLA Ops:
  0.6 121.6 %shard_map.103 = (f32[1,256]{1,0:T(1,128)}, bf16[320,256]{1,0:T(8,128)(2,1)}, f32[8,512]{1,0:T(8,128)}) custom-call(bf16[320,256]{1,0:T(8,128)(2,1)} %bitcast.6, bf16[320,256]{1,0:T(8,128)(2,1)} %bitcast.7, bf16[320,512]{1,0:T(8,128)(2,1)} %wg.1, bf16[320,512]{1,0:T(8,128)(2,1)} %wu.1, bf16[320,512]{1,0:T(8,128)(2,1)} %wd.1, bf16[16,320,128]{2,1,0:T(8,128)(2,1)} %bitcast.5, ...), custom_call_target="tpu_custom_call" | custom-call | tf_op jit(solution)/shard_map/pallas_call | solution.py:642
  122.3 1.6 %shard_map.104 = (f32[256]{0:T(256)}, bf16[320,256]{1,0:T(8,128)(2,1)}, f32[8,512]{1,0:T(8,128)}) custom-call(f32[1,256]{1,0:T(1,128)} %get-tuple-element.9.lr_in, bf16[320,256]{1,0:T(8,128)(2,1)} %get-tuple-element.10.ig_in, f32[8,512]{1,0:T(8,128)} %get-tuple-element.11.abg_in), custom_call_target="tpu_custom_call" | custom-call | tf_op jit(solution)/shard_map/pallas_call | solution.py:710

commit v6 on v5

--- a/solution.py
+++ b/solution.py
@@ -508,9 +508,9 @@
             @pl.when(j == e)
             def _():
                 after(e)
-                if e == 1:
+                if e == 2:
                     log_ratios()
-                if e == 5:
+                if e == 6:
                     coefficients()
         return carry
 

time: 124 us -> 124 us (level)
  no operation moved by 1% of the time
where the time goes in v6:
time: 124 us
  Pallas kernels  123 us (99%)
    pallas_call x1, Pallas kernels, on_device(): pl.pallas_call(kernel, out_shape=(jax.ShapeDtypeStruct((1, ROWS), F32), j...  122 us

profile of v6, /device:TPU:1, one launch (start us, length us, event | category | flops | bytes accessed | tf_op | source)
XLA Modules:
  0.0 123.8 jit_solution(5190323347099201544)
XLA Ops:
  0.6 121.6 %shard_map.103 = (f32[1,256]{1,0:T(1,128)}, bf16[320,256]{1,0:T(8,128)(2,1)}, f32[8,512]{1,0:T(8,128)}) custom-call(bf16[320,256]{1,0:T(8,128)(2,1)} %bitcast.6, bf16[320,256]{1,0:T(8,128)(2,1)} %bitcast.7, bf16[320,512]{1,0:T(8,128)(2,1)} %wg.1, bf16[320,512]{1,0:T(8,128)(2,1)} %wu.1, bf16[320,512]{1,0:T(8,128)(2,1)} %wd.1, bf16[16,320,128]{2,1,0:T(8,128)(2,1)} %bitcast.5, ...), custom_call_target="tpu_custom_call" | custom-call | tf_op jit(solution)/shard_map/pallas_call | solution.py:642
  122.2 1.6 %shard_map.104 = (f32[256]{0:T(256)}, bf16[320,256]{1,0:T(8,128)(2,1)}, f32[8,512]{1,0:T(8,128)}) custom-call(f32[1,256]{1,0:T(1,128)} %get-tuple-element.9.lr_in, bf16[320,256]{1,0:T(8,128)(2,1)} %get-tuple-element.10.ig_in, f32[8,512]{1,0:T(8,128)} %get-tuple-element.11.abg_in), custom_call_target="tpu_custom_call" | custom-call | tf_op jit(solution)/shard_map/pallas_call | solution.py:710
